TPU v7x, 256 devices: a whole 4x4x8 slice. The times are simulated.
256 devices in a mesh: row: 8 (over z_hi, x), col: 32 (over z_lo, y, core).
Axes of the slice: x: 4, y: 4, z: 8 (z_hi: 2, z_lo: 4; z = z_hi * 4 + z_lo), core: 2. Of those that a mesh axis runs over, the one named last changes fastest.
Arguments:
- acts: bfloat16 [65536, 5120], P(('row', 'col')), may hold values from -24 to 24
- outgrads: bfloat16 [65536, 8192], P(('row', 'col')), may hold values from -24 to 24
- weight_grad: float32 [5120, 8192], P('row', 'col'), may hold values from -24 to 24
- prev_factor: float32 [256, 128, 128], P(('row', 'col')), as said below
- damping: float32 [], replicated, may hold values from 1 to 4
- block_slot_owner: int32 [256], replicated, may hold values from 0 to 255, each once
Outputs:
- precond_grad: float32 [5120, 8192], P('row', 'col')
- updated_factor_blocks: float32 [256, 128, 128], P(('row', 'col'))
Inputs may be any that keep to these rules, and one draw needn't show every extreme that they name: `block_slot_owner`: A permutation of the 256 slots; only entries 0 to 103 name blocks' slots. `prev_factor`: symmetric blocks.
All inputs are finite; a program needn't handle non-finite values. Where the computation divides by a largest or mean magnitude, that divisor is 1e-20 or more.
Results may differ from a plain program's by a relative error of at most 0.0003.
Values sent between devices are 32-bit elements; how exact they have to be, the bound alone decides.
No kernel may reach another device: no remote copies, remote signals or barrier semaphores. Data moves between devices by JAX's collectives and lax.ppermute only.
A program may use at most 128 MiB of HBM per device.

v0:
```python
import jax
import jax.numpy as jnp
from jax import lax
from jax.sharding import PartitionSpec as P

D = 5120
H = 8192
BLOCK_ORDER = 128
ITERS = 6


ema_decay = 0.8


def invert(blocks, damp):
    eye = jnp.eye(blocks.shape[-1], dtype=jnp.float32)
    damped = blocks + damp * eye
    bound = jnp.max(jnp.sum(jnp.abs(damped), axis=2), axis=1)
    approx = eye[None] / bound[:, None, None]
    for step in range(ITERS):
        product = jnp.einsum("bij,bjk->bik", damped, approx, precision=lax.Precision.HIGHEST)
        approx = jnp.einsum(
            "bij,bjk->bik", approx, 2.0 * eye - product, precision=lax.Precision.HIGHEST
        )
    return approx


def block_partial(data):
    count = data.shape[1] // BLOCK_ORDER
    shaped = data.reshape(data.shape[0], count, BLOCK_ORDER)
    return jnp.einsum("tbi,tbj->bij", shaped, shaped, preferred_element_type=jnp.float32)


def apply_both(weight_grad, left_inverse, right_inverse):
    rows_here = weight_grad.shape[0] // BLOCK_ORDER
    cols_here = weight_grad.shape[1] // BLOCK_ORDER
    tiles = weight_grad.reshape(rows_here, BLOCK_ORDER, cols_here, BLOCK_ORDER)
    left = jnp.einsum("kij,kjlm->kilm", left_inverse, tiles, precision=lax.Precision.HIGHEST)
    both = jnp.einsum("kilm,lmn->kiln", left, right_inverse, precision=lax.Precision.HIGHEST)
    return both.reshape(weight_grad.shape)


def on_device(acts, outgrads, weight_grad, prev_factor, damping, block_slot_owner):
    devices = lax.axis_size(("row", "col"))
    me = lax.axis_index(("row", "col"))
    slots_dev = prev_factor.shape[0]
    slot_total = slots_dev * devices
    tokens_all = acts.shape[0] * devices
    blocks_a = D // BLOCK_ORDER
    blocks_all = blocks_a + H // BLOCK_ORDER
    rows_here = weight_grad.shape[0] // BLOCK_ORDER
    cols_here = weight_grad.shape[1] // BLOCK_ORDER
    partial_blocks = jnp.concatenate([block_partial(acts), block_partial(outgrads)], axis=0)
    owner_slots = block_slot_owner[:blocks_all]
    matches = owner_slots[None, :] == jnp.arange(slot_total, dtype=jnp.int32)[:, None]
    slot_block = jnp.sum(
        jnp.where(matches, jnp.arange(blocks_all, dtype=jnp.int32)[None, :], 0), axis=1
    )
    slot_used = jnp.any(matches, axis=1)
    my_used = lax.dynamic_slice_in_dim(slot_used, me * slots_dev, slots_dev, 0)
    my_blocks = lax.dynamic_slice_in_dim(slot_block, me * slots_dev, slots_dev, 0)
    summed = lax.psum(partial_blocks, ("row", "col"))
    mine = jnp.take(summed, my_blocks, axis=0)
    batch = mine / tokens_all
    fresh_factor = ema_decay * prev_factor + (1.0 - ema_decay) * batch
    updated_factor_blocks = jnp.where(my_used[:, None, None], fresh_factor, 0.0)
    inverse = invert(updated_factor_blocks, damping)
    every_inverse = lax.all_gather(inverse, ("row", "col"), axis=0, tiled=True)
    row_ids = lax.dynamic_slice_in_dim(
        block_slot_owner, lax.axis_index("row") * rows_here, rows_here, 0
    )
    col_ids = lax.dynamic_slice_in_dim(
        block_slot_owner, blocks_a + lax.axis_index("col") * cols_here, cols_here, 0
    )
    left_inverse = jnp.take(every_inverse, row_ids, axis=0)
    right_inverse = jnp.take(every_inverse, col_ids, axis=0)
    return (apply_both(weight_grad, left_inverse, right_inverse), updated_factor_blocks)


def solution(mesh):
    placed = (
        P(("row", "col"), None),
        P(("row", "col"), None),
        P("row", "col"),
        P(("row", "col"), None, None),
        P(),
        P(),
    )
    return jax.shard_map(
        on_device,
        mesh=mesh,
        in_specs=placed,
        out_specs=(P("row", "col"), P(("row", "col"), None, None)),
        check_vma=False,
    )
```

profile of v0, /device:TPU:1, one launch (start us, length us, event | category | flops | bytes accessed | tf_op | source)
XLA Modules:
  0.0 755.8 jit_solution(6195853386947773756)
XLA Ops:
  7.2 0.0 copy-start
  7.2 0.0 all-reduce.2.cloned.1.call-start
  7.2 1.7 copy-done
  8.9 0.0 copy-start.1
  8.9 0.9 fusion.3
  9.8 1.3 copy-done.1
  11.1 1.4 fusion
  12.5 3.7 pad_maximum_fusion
  16.2 0.0 copy-start.4
  16.2 0.0 copy-start.3
  16.2 0.0 all-reduce.2.cloned.1.call-update
  16.2 0.0 all-gather.3.cloned.1.call-start
  16.9 0.0 copy-done.4
  17.0 0.1 fusion.14
  17.1 0.6 dynamic_slice.13
  17.7 0.1 select_reduce_fusion
  17.8 0.6 dynamic_slice.14
  20.3 273.7 %all-reduce.2.cloned.1.call-done = f32[104,128,128]{2,1,0:T(8,128)} async-done(((f32[104,128,128]{2,1,0:T(8,128)}), f32[104,128,128]{2,1,0:T(8,128)}) %all-reduce.2.cloned.1.call-update) | async-done | bytes 6815760 | tf_op jit(solution)/shard_map/psum | solution.py:62
  294.0 0.0 copy-done.3
  294.0 1.5 abs_reduce_fusion
  295.5 0.0 copy-start.2
  295.6 0.6 reduce_max.9
  296.9 0.2 convolution_subtract_fusion.5
  297.1 0.2 fusion.15
  297.3 0.2 convolution_subtract_fusion.4
  297.5 0.2 fusion.38
  297.7 0.2 convolution_subtract_fusion.3
  297.9 0.2 fusion.39
  298.1 0.2 convolution_subtract_fusion.2
  298.3 0.2 fusion.40
  298.6 0.2 convolution_subtract_fusion.1
  298.8 0.2 fusion.41
  299.0 0.2 convolution_subtract_fusion
  299.2 0.8 fusion.42
  300.0 0.0 all-gather.3.cloned.1.call-update
  300.1 1.4 reshape.131
  301.5 0.1 compare_and_fusion.1
  301.6 0.1 compare_and_fusion
  301.7 428.1 %all-gather.3.cloned.1.call-done = f32[32768,128]{1,0:T(8,128)} async-done(((f32[128,128]{1,0:T(8,128)}), f32[32768,128]{1,0:T(8,128)}) %all-gather.3.cloned.1.call-update) | async-done | bytes 16777232 | tf_op jit(solution)/shard_map/all_gather | solution.py:68
  729.8 6.3 gather_fusion
  736.1 7.1 gather_fusion.1
  743.2 1.7 fusion.6
  744.9 0.9 convolution_bitcast_fusion
  745.8 1.2 copy.24
  747.0 0.0 copy-done.2
  747.0 2.0 copy.42
  (3 shorter events, 0.0 us)
Async XLA Ops:
  7.2 1.7 copy-start
  7.2 286.8 %all-reduce.2.cloned.1.call-start = ((), (), s32[]{:S(2)}) async-start(), calls=%async_computation | async-start | bytes 13631488 | tf_op jit(solution)/shard_map/psum | solution.py:62
  8.9 2.2 copy-start.1
  16.2 0.7 copy-start.4
  16.2 277.8 %copy-start.3 = (f32[1,128,128]{2,1,0:T(8,128)S(1)}, f32[1,128,128]{2,1,0:T(8,128)}, u32[]{:S(2)}) copy-start(f32[1,128,128]{2,1,0:T(8,128)} %param.9) | copy-start | bytes 196612
  16.2 713.5 %all-gather.3.cloned.1.call-start = ((), (), s32[]{:S(2)}) async-start(), calls=%async_computation.1 | async-start | bytes 16842752 | tf_op jit(solution)/shard_map/all_gather | solution.py:68
  295.5 451.5 %copy-start.2 = (f32[1,128,128]{2,1,0:T(8,128)}, f32[1,128,128]{2,1,0:T(8,128)S(1)}, u32[]{:S(2)}) copy-start(f32[1,128,128]{2,1,0:T(8,128)S(1)} %get-tuple-element.18) | copy-start | bytes 196612
Sparse Core Ops, SparseCore 0:
  16.4 277.6 all-reduce.1
  300.2 429.5 all-gather.2
where the time goes:
time: 757 us; the launch traced here: 756 us
  waiting for transfers between devices  702 us (93%)
  local copies, waits for them, and re-layouts  22.1 us (3%)
  between operations  17.5 us (2%)
  matrix products  8.04 us (1%)
    all_gather x1, waiting for transfers between devices, on_device(): every_inverse = lax.all_gather(inverse, ('row', 'col'), axis=0, tiled=True)  428 us
    psum x1, waiting for transfers between devices, on_device(): summed = lax.psum(partial_blocks, ('row', 'col'))  274 us
  transfers between devices with their start and end apart: 2, of which 2 were waited for; matrix products, arithmetic and copies ran while one was open for 0% of the time, Pallas kernels for 0%

commit v1 on v0

v1 whole, which is shorter than its diff:
```python
import functools

import jax
import jax.numpy as jnp
import numpy as np
from jax import lax
from jax.experimental import pallas as pl
from jax.experimental.pallas import tpu as pltpu
from jax.sharding import Mesh
from jax.sharding import PartitionSpec as P

D = 5120
H = 8192
N = 128
ITERS = 6
TOKENS = 65536
NA = D // N
NB = NA + H // N
SLOTS = 256

ema_decay = 0.8

HALF = 26
TILES = HALF + 1
ALL = ("zh", "x", "zl", "y", "c")
PLANE = ("x", "y")
DEPTH = ("zh", "zl")
SPREAD = ("c", "x", "y", "zh", "zl")


def pair_home(block):
    group, at = block // 10, (block % 10) // 2
    col = (block - NA) // 2
    last = at == 2
    high = at > 2
    a_half = jnp.where(last, group % 2, jnp.where(high, at - 3, at))
    a_place = jnp.where(last, 8 + group // 2, jnp.where(high, group + 4, group))
    is_a = block < NA
    return jnp.where(is_a, a_half, col % 2), jnp.where(is_a, a_place, 10 + col // 2)


def pair_column(place, half):
    if place < 8:
        return 0, 5 * (place % 4) + (3 if place >= 4 else 0) + half
    if place < 10:
        return 0, 5 * (half + 2 * (place - 8)) + 2
    return 1, 2 * (place - 10) + half


def lower_mask():
    r = lax.broadcasted_iota(jnp.int32, (N, N), 0)
    c = lax.broadcasted_iota(jnp.int32, (N, N), 1)
    return r, c


SCALE = (1.0 - ema_decay) / TOKENS


def gram(x):
    return lax.dot_general(x, x, (((0,), (0,)), ((), ())), preferred_element_type=jnp.float32)


def partial_kernel(own, meta, acts, outgrads, prev, diag_in, out, diag_out, buf, odd, rows, sems, odd_sems):
    half = meta[0]
    copies, odd_copies = [], []
    for place in range(HALF):
        which, pair = pair_column(place, half)
        src = outgrads if which else acts
        off = pl.multiple_of(pair * (2 * N), 2 * N)
        copies.append(pltpu.make_async_copy(src.at[:, pl.ds(off, 2 * N)], buf.at[place], sems.at[place]))
        copies[-1].start()
    if not own:
        for place in range(HALF):
            which, pair = pair_column(place, 1 - half)
            src = outgrads if which else acts
            off = pl.multiple_of(pair * (2 * N) + N, N)
            odd_copies.append(
                pltpu.make_async_copy(src.at[:, pl.ds(off, N)], odd.at[place], odd_sems.at[place])
            )
            odd_copies[-1].start()
        rows[...] = jnp.zeros((N, N), jnp.float32)
    r, c = lower_mask()
    for place in range(HALF):
        copies[place].wait()
        first = gram(buf[place, :, :N])
        second = gram(buf[place, :, N:])
        packed = jnp.where(r <= c, first, second) * SCALE
        out[:, place] = packed.reshape(16, 8, N)
        if not own:
            line = jnp.sum(jnp.where(r == c, second, 0.0), axis=0, keepdims=True)
            rows[pl.ds(32 * half + place, 1), :] = line * SCALE
    if not own:
        for place in range(HALF):
            odd_copies[place].wait()
            x = odd[place].astype(jnp.float32)
            rows[pl.ds(32 * (1 - half) + place, 1), :] = jnp.sum(x * x, axis=0, keepdims=True) * SCALE

    block, slot_half, place, second_of = meta[1], meta[2], meta[3], meta[4]

    @pl.when((block > 0) & (slot_half == half))
    def _():
        mine = jnp.where((r > c) == (second_of == 1), prev[0] * ema_decay, 0.0)
        out[:, place] += mine.reshape(16, 8, N)

    if own:
        out[:, HALF] = diag_in[...]
    else:

        @pl.when((block > 0) & (second_of == 1))
        def _():
            line = jnp.sum(jnp.where(r == c, prev[0], 0.0), axis=0, keepdims=True)
            rows[pl.ds(32 * slot_half + place, 1), :] += line * ema_decay

        diag = rows[...].T.reshape(16, 8, N)
        diag_out[...] = diag
        out[:, HALF] = diag


def partials(meta, acts, outgrads, prev, diag=None):
    own = diag is not None
    shape = jax.ShapeDtypeStruct((16, TILES, 8, N), jnp.float32)
    diag_shape = jax.ShapeDtypeStruct((16, 8, N), jnp.float32)
    vmem = pl.BlockSpec(memory_space=pltpu.VMEM)
    hbm = pl.BlockSpec(memory_space=pl.ANY)
    scratch = [pltpu.VMEM((HALF, 256, 2 * N), jnp.bfloat16)]
    if own:

        def kernel(meta, acts, outgrads, prev, diag_in, out, buf, sems):
            partial_kernel(True, meta, acts, outgrads, prev, diag_in, out, None, buf, None, None, sems, None)

        scratch += [pltpu.SemaphoreType.DMA((HALF,))]
    else:

        def kernel(meta, acts, outgrads, prev, out, diag_out, buf, odd, rows, sems, odd_sems):
            partial_kernel(
                False, meta, acts, outgrads, prev, None, out, diag_out, buf, odd, rows, sems, odd_sems
            )

        scratch += [
            pltpu.VMEM((HALF, 256, N), jnp.bfloat16),
            pltpu.VMEM((N, N), jnp.float32),
            pltpu.SemaphoreType.DMA((HALF,)),
            pltpu.SemaphoreType.DMA((HALF,)),
        ]
    return pl.pallas_call(
        kernel,
        out_shape=shape if own else (shape, diag_shape),
        in_specs=[pl.BlockSpec(memory_space=pltpu.SMEM), hbm, hbm, vmem] + ([vmem] if own else []),
        out_specs=vmem if own else (vmem, vmem),
        scratch_shapes=scratch,
        compiler_params=pltpu.CompilerParams(vmem_limit_bytes=40 * 2**20),
        name="own_half" if own else "other_half",
    )(*((meta, acts, outgrads, prev) + ((diag,) if own else ())))


def plane_kernel(got, out, total):
    for tile in range(TILES):
        parts = [got[s, tile] for s in range(16)]
        while len(parts) > 1:
            parts = [a + b for a, b in zip(parts[::2], parts[1::2])]
        total[pl.ds(8 * tile, 8), :] = parts[0]
    total[pl.ds(8 * TILES, 40), :] = jnp.zeros((40, N), jnp.float32)
    for z in range(8):
        out[z] = total[pl.ds(z, 32, stride=8), :]


def plane_sum(got):
    return pl.pallas_call(
        plane_kernel,
        out_shape=jax.ShapeDtypeStruct((8, 32, N), jnp.float32),
        in_specs=[pl.BlockSpec(memory_space=pltpu.VMEM)],
        out_specs=pl.BlockSpec(memory_space=pltpu.VMEM),
        scratch_shapes=[pltpu.VMEM((256, N), jnp.float32)],
        compiler_params=pltpu.CompilerParams(vmem_limit_bytes=40 * 2**20),
        name="plane_sum",
    )(got)


def thirds(x):
    high = x.astype(jnp.bfloat16)
    rest = x - high.astype(jnp.float32)
    mid = rest.astype(jnp.bfloat16)
    low = (rest - mid.astype(jnp.float32)).astype(jnp.bfloat16)
    return high, mid, low


def spread_kernel(got, picks, out):
    total = got[0]
    for z in range(1, 8):
        total = total + got[z]
    stacked = jnp.concatenate(thirds(total), axis=0)
    out[...] = jnp.dot(picks[...], stacked, preferred_element_type=jnp.float32)


def spread_rows(got, picks):
    return pl.pallas_call(
        spread_kernel,
        out_shape=jax.ShapeDtypeStruct((4 * SLOTS, N), jnp.float32),
        in_specs=[pl.BlockSpec(memory_space=pltpu.VMEM)] * 2,
        out_specs=pl.BlockSpec(memory_space=pltpu.VMEM),
        compiler_params=pltpu.CompilerParams(vmem_limit_bytes=40 * 2**20),
        name="spread_rows",
    )(got, picks)


def left_form(a):
    a1, a2, a3 = thirds(a)
    return jnp.concatenate([a1, a2], axis=1), jnp.concatenate([a1, a3], axis=1)


def mul(left, b):
    b1, b2, b3 = thirds(b)
    wide = jnp.concatenate(
        [jnp.concatenate([b1, b2], axis=1), jnp.concatenate([b2, b1], axis=1)], axis=0
    )
    main = jnp.dot(left[0], wide, preferred_element_type=jnp.float32)
    small = jnp.dot(left[1], jnp.concatenate([b3, b1], axis=0), preferred_element_type=jnp.float32)
    return main[:, :N] + (main[:, N:] + small)


def apply_kernel(meta, got, damping, weight, out, updated, left_out):
    core, row, col = meta[0], meta[1], meta[2]
    block, slot_half, slot_place, slot_second = meta[3], meta[4], meta[5], meta[6]
    group, odd_row = row // 2, row % 2
    r, c = lower_mask()
    lower, on = r > c, r == c
    eye = jnp.where(on, 1.0, 0.0)

    def fetch(half, k):
        return got[pl.ds(half * 512 + k, N, stride=4), :]

    diags = fetch(1 - core, 2)

    def block_of(packed, flipped, second, lane):
        column = jnp.sum(jnp.where(c == lane, diags, 0.0), axis=1, keepdims=True)
        if isinstance(second, int):
            if second == 0:
                return jnp.where(lower, flipped, packed)
            return jnp.where(on, column, jnp.where(lower, packed, flipped))
        straight = jnp.where(lower, second, 1 - second) == 1
        return jnp.where(on & (second == 1), column, jnp.where(straight, packed, flipped))

    blocks = []
    for half in range(2):
        packed = fetch(half, 0)
        flipped = packed.T
        lane = 32 * half + group + 4 * odd_row
        blocks += [block_of(packed, flipped, second, lane) for second in range(2)]
    packed = fetch(group % 2, 1)
    blocks.append(block_of(packed, packed.T, odd_row, 32 * (group % 2) + 8 + group // 2))
    packed = fetch(core, 2)
    flipped = packed.T
    blocks += [block_of(packed, flipped, second, 32 * core + 10 + col // 2) for second in range(2)]
    packed = fetch(slot_half, 3)
    fresh = block_of(packed, packed.T, slot_second, 32 * slot_half + slot_place)
    updated[0] = jnp.where(block > 0, fresh, 0.0)

    damped, approx = [], []
    for one in blocks:
        one = one + damping[0] * eye
        bound = jnp.max(jnp.sum(jnp.abs(one), axis=0, keepdims=True), axis=1, keepdims=True)
        start = 1.0 / bound
        damped.append(left_form(one))
        approx.append((2.0 * eye - one * start) * start)
    for _ in range(ITERS - 1):
        rest = [2.0 * eye - mul(d, x) for d, x in zip(damped, approx)]
        approx = [mul(left_form(x), y) for x, y in zip(approx, rest)]

    for i in range(5):
        place = jnp.where(odd_row == 1, (i + 1) % 5, i)
        at = pl.ds(pl.multiple_of(place * N, N), N)
        a = left_form(approx[i])
        w1, w2, w3 = thirds(weight[at, :])
        main = jnp.dot(a[0], jnp.concatenate([w1, w1], axis=0), preferred_element_type=jnp.float32)
        a1, a2 = a[0][:, :N], a[0][:, N:]
        a3 = a[1][:, N:]
        cross = jnp.dot(a[0], jnp.concatenate([w2, w2], axis=0), preferred_element_type=jnp.float32)
        small = jnp.dot(
            jnp.concatenate([a1, a3], axis=1),
            jnp.concatenate([w3, w1], axis=0),
            preferred_element_type=jnp.float32,
        )
        left_out[at, :] = main + (cross + small)
    for j in range(2):
        at = slice(j * N, (j + 1) * N)
        out[:, at] = mul(left_form(left_out[:, at]), approx[5 + j])


def apply_all(meta, got, damping, weight):
    vmem = pl.BlockSpec(memory_space=pltpu.VMEM)
    smem = pl.BlockSpec(memory_space=pltpu.SMEM)
    return pl.pallas_call(
        apply_kernel,
        out_shape=(
            jax.ShapeDtypeStruct(weight.shape, jnp.float32),
            jax.ShapeDtypeStruct((1, N, N), jnp.float32),
        ),
        in_specs=[smem, vmem, smem, vmem],
        out_specs=(vmem, vmem),
        scratch_shapes=[pltpu.VMEM(weight.shape, jnp.float32)],
        compiler_params=pltpu.CompilerParams(vmem_limit_bytes=40 * 2**20),
        name="invert_apply",
    )(meta, got, damping, weight)


def destinations():
    c, x, y, zh, zl = np.unravel_index(np.arange(SLOTS), (2, 4, 4, 2, 4))
    row, col = zh * 4 + x, (zl * 4 + y) * 2 + c
    return c, row, col, row * 32 + col


def picked_rows(owner, half):
    core, row, col, slot = destinations()
    group, odd_row = row // 2, row % 2
    first = group + 4 * odd_row
    second = 8 + group // 2
    third = jnp.where(jnp.asarray(core) == half, jnp.asarray(10 + col // 2), HALF)
    halves, places = pair_home(jnp.arange(NB, dtype=jnp.int32))
    matches = (owner[:NB, None] == jnp.asarray(slot, jnp.int32)[None, :]) & (halves == half)[:, None]
    fourth = jnp.sum(jnp.where(matches, places[:, None], 0), axis=0)
    rows = jnp.stack([jnp.asarray(first), jnp.asarray(second), third, fourth], axis=1).astype(jnp.int32)
    wanted = jnp.arange(96, dtype=jnp.int32) % 32
    return (rows[:, :, None] == wanted).astype(jnp.bfloat16).reshape(4 * SLOTS, 96)


def on_device(acts, outgrads, weight_grad, prev_factor, damping, owner):
    core = lax.axis_index("c").astype(jnp.int32)
    row = lax.axis_index(("zh", "x")).astype(jnp.int32)
    col = lax.axis_index(("zl", "y", "c")).astype(jnp.int32)
    me = row * 32 + col
    numbers = jnp.arange(NB, dtype=jnp.int32)
    block = jnp.sum(jnp.where(owner[:NB] == me, numbers + 1, 0))
    slot_half, slot_place = pair_home(jnp.maximum(block - 1, 0))
    slot_second = jnp.maximum(block - 1, 0) % 2
    slot = [block, slot_half, slot_place, slot_second]
    other_meta = jnp.stack([1 - core] + slot).astype(jnp.int32)
    own_meta = jnp.stack([core] + slot).astype(jnp.int32)
    apply_meta = jnp.stack([core, row, col] + slot).astype(jnp.int32)
    picks = picked_rows(owner, core)

    other, diag = partials(other_meta, acts, outgrads, prev_factor)
    received = lax.ppermute(other, "c", [(0, 1), (1, 0)])
    own = partials(own_meta, acts, outgrads, prev_factor, diag)
    chip = own + received
    got = lax.all_to_all(chip, PLANE, 0, 0, tiled=True)
    by_depth = plane_sum(got)
    got = lax.all_to_all(by_depth, DEPTH, 0, 0, tiled=True)
    sent = spread_rows(got, picks)
    got = lax.all_to_all(sent.reshape(SLOTS, 4, N), SPREAD, 0, 0, tiled=True)
    return apply_all(apply_meta, got.reshape(4 * SLOTS, N), damping.reshape(1), weight_grad)


def solution(mesh):
    fine = Mesh(mesh.devices.reshape(2, 4, 4, 4, 2), ALL)
    row, col = ("zh", "x"), ("zl", "y", "c")
    placed = (P(ALL, None), P(ALL, None), P(row, col), P(ALL, None, None), P(), P())
    return jax.shard_map(
        on_device,
        mesh=fine,
        in_specs=placed,
        out_specs=(P(row, col), P(ALL, None, None)),
        check_vma=False,
    )
```

time: 757 us -> 119 us (0.16)
  waiting for transfers between devices: 702 us -> 52.9 us
  Pallas kernels: 0 us -> 24.8 us
  starting transfers between devices: 0.08 us -> 24.7 us
  between operations: 17.5 us -> 2.28 us
  local copies, waits for them, and re-layouts: 22.1 us -> 9.56 us
  matrix products: 8.04 us -> 0 us
    all_gather x1 -> x0, waiting for transfers between devices: 428 us -> none  [on_device(): every_inverse = lax.all_gather(inverse, ('row', 'col'), axis=0, tiled=True)]
    psum x1 -> x0, waiting for transfers between devices: 274 us -> none  [on_device(): summed = lax.psum(partial_blocks, ('row', 'col'))]
    all_to_all x0 -> x3, waiting for transfers between devices: none -> 52.9 us  [the longest x1 25.2 us: on_device(): got = lax.all_to_all(chip, PLANE, 0, 0, tiled=True)]
    pallas_call x0 -> x5, Pallas kernels: none -> 24.8 us  [the longest x2 17.8 us: partials(): pl.pallas_call(kernel, out_shape=shape if own else (shape, diag_shape), i...]
    all_to_all x0 -> x3, starting transfers between devices: none -> 21.4 us  [the longest x1 8.17 us: on_device(): got = lax.all_to_all(by_depth, DEPTH, 0, 0, tiled=True)]
    gather x2 -> x0, local copies, waits for them, and re-layouts: 13.4 us -> none  [the longest x1 7.06 us: on_device(): left_inverse = jnp.take(every_inverse, row_ids, axis=0)]
    dot_general x16 -> x0, matrix products: 8.04 us -> none  [the longest x2 2.34 us: block_partial(): jnp.einsum('tbi,tbj->bij', shaped, shaped, preferred_element_type=jnp.flo...]
  transfers between devices with their start and end apart: 2 -> 4, of which waited for: 2 -> 3; matrix products, arithmetic and copies ran while one was open for 0% -> 2% of each run, Pallas kernels for 0% -> 6%
where the time goes in v1:
time: 119 us
  waiting for transfers between devices  52.9 us (44%)
  Pallas kernels  24.8 us (21%)
  starting transfers between devices  24.7 us (21%)
  local copies, waits for them, and re-layouts  9.56 us (8%)
  other arithmetic  4.63 us (4%)
  between operations  2.28 us (2%)
    all_to_all x1, waiting for transfers between devices, on_device(): got = lax.all_to_all(chip, PLANE, 0, 0, tiled=True)  25.2 us
    all_to_all x1, waiting for transfers between devices, on_device(): got = lax.all_to_all(sent.reshape(SLOTS, 4, N), SPREAD, 0, 0, tiled=True)  19.9 us
    pallas_call x2, Pallas kernels, partials(): pl.pallas_call(kernel, out_shape=shape if own else (shape, diag_shape), i...  17.8 us
    all_to_all x1, starting transfers between devices, on_device(): got = lax.all_to_all(by_depth, DEPTH, 0, 0, tiled=True)  8.17 us
    all_to_all x1, starting transfers between devices, on_device(): got = lax.all_to_all(sent.reshape(SLOTS, 4, N), SPREAD, 0, 0, tiled=True)  8.11 us
    all_to_all x1, waiting for transfers between devices, on_device(): got = lax.all_to_all(by_depth, DEPTH, 0, 0, tiled=True)  7.82 us
    unnamed x24, local copies, waits for them, and re-layouts  6.99 us
    pallas_call x1, Pallas kernels, apply_all(): pl.pallas_call(apply_kernel, out_shape=(jax.ShapeDtypeStruct(weight.shape...  5.26 us
  transfers between devices with their start and end apart: 4, of which 3 were waited for; matrix products, arithmetic and copies ran while one was open for 2% of the time, Pallas kernels for 6%

profile of v1, /device:TPU:1, one launch (start us, length us, event | category | flops | bytes accessed | tf_op | source)
XLA Modules:
  0.0 118.9 jit_solution(15629733852080490639)
XLA Ops:
  0.6 1.4 %fusion.5 = (s32[104]{0:T(128)S(1)}, s32[]{:T(128)}, s32[104]{0:T(128)S(1)}) fusion(s32[256]{0:T(256)} %param.16, s32[]{:T(128)S(6)} %add.170), kind=kLoop, calls=%fused_computation.40 | loop fusion | flops 8943 | bytes 1256 | tf_op jit(solution)/shard_map/slice | solution.py:332
  2.9 0.8 stack.67.meta
  3.7 0.0 copy-start
  3.7 2.2 %copy-done = bf16[256,8192]{1,0:T(8,128)(2,1)S(1)} copy-done((bf16[256,8192]{1,0:T(8,128)(2,1)S(1)}, bf16[256,8192]{1,0:T(8,128)(2,1)}, u32[]{:S(2)}) %copy-start) | copy-done | bytes 4194328
  5.8 0.0 copy-start.2
  5.8 1.7 %copy-done.2 = bf16[256,5120]{1,0:T(8,128)(2,1)S(1)} copy-done((bf16[256,5120]{1,0:T(8,128)(2,1)S(1)}, bf16[256,5120]{1,0:T(8,128)(2,1)}, u32[]{:S(2)}) %copy-start.2) | copy-done | bytes 2621464
  7.6 0.0 copy-start.5
  7.6 0.8 copy-done.5
  8.4 0.0 copy-start.3
  8.4 0.0 copy-start.6
  8.4 10.4 %other_half.1 = (f32[16,27,8,128]{3,2,1,0:T(8,128)}, f32[16,8,128]{2,1,0:T(8,128)S(1)}) custom-call(s32[5]{0:T(128)S(1)} %stack.67.meta, bf16[256,5120]{1,0:T(8,128)(2,1)S(1)} %copy-done.2, bf16[256,8192]{1,0:T(8,128)(2,1)S(1)} %copy-done, f32[1,128,128]{2,1,0:T(8,128)S(1)} %copy-done.5), custom_call_target="tpu_custom_call" | custom-call | tf_op jit(solution)/shard_map/other_half/pallas_call | solution.py:145
  18.9 3.3 %collective-permute-start = (f32[16,27,8,128]{3,2,1,0:T(8,128)}, f32[16,27,8,128]{3,2,1,0:T(8,128)}, u32[]{:S(2)}, u32[]{:S(2)}) collective-permute-start(f32[16,27,8,128]{3,2,1,0:T(8,128)} %get-tuple-element.5), channel_id=1, source_target_pairs={{0,1},{1,0},{2,3},{3,2},{4,5},{5,4},{6,7},{7,6},{8,9},{9,8},{10,11... | collective-permute-start | bytes 5308424 | tf_op jit(solution)/shard_map/ppermute | solution.py:342
  22.2 0.8 stack.65.meta
  23.0 0.0 copy-done.3
  23.0 0.0 copy-done.6
  23.0 0.0 copy-start.1
  23.0 2.2 %copy-done.1 = bf16[256,8192]{1,0:T(8,128)(2,1)S(1)} copy-done((bf16[256,8192]{1,0:T(8,128)(2,1)S(1)}, bf16[256,8192]{1,0:T(8,128)(2,1)}, u32[]{:S(2)}) %copy-start.1) | copy-done | bytes 4194328
  25.2 7.3 %own_half.1 = f32[16,27,8,128]{3,2,1,0:T(8,128)S(1)} custom-call(s32[5]{0:T(128)S(1)} %stack.65.meta, bf16[256,5120]{1,0:T(8,128)(2,1)S(1)} %copy-done.3, bf16[256,8192]{1,0:T(8,128)(2,1)S(1)} %copy-done.1, f32[1,128,128]{2,1,0:T(8,128)S(1)} %copy-done.6, f32[16,8,128]{2,1,0:T(8,128)S(1)} %get-tuple-element.4.diag_in), custom_call_target="tpu_custom_call" | custom-call | tf_op jit(solution)/shard_map/own_half/pallas_call | solution.py:145
  32.5 0.0 collective-permute-done
  32.5 2.9 %add.180 = f32[16,27,8,128]{3,2,1,0:T(8,128)} add(f32[16,27,8,128]{3,2,1,0:T(8,128)S(1)} %own_half.1, f32[16,27,8,128]{3,2,1,0:T(8,128)} %collective-permute-done) | non-fusion elementwise | flops 442368 | bytes 5308416 | tf_op jit(solution)/shard_map/add | solution.py:344
  35.4 0.0 copy-start.9
  35.4 0.0 copy-start.7
  35.4 0.0 copy-start.8
  35.4 0.0 copy-start.10
  35.4 0.0 copy-start.11
  35.4 5.1 %all-to-all-start = ((f32[16,27,8,128]{3,2,1,0:T(8,128)}), f32[16,27,8,128]{3,2,1,0:T(8,128)S(1)}, u32[]{:S(2)}, u32[]{:S(2)}) async-start(f32[16,27,8,128]{3,2,1,0:T(8,128)} %add.180), calls=%async_computation | async-start | bytes 3538944 | tf_op jit(solution)/shard_map/all_to_all | solution.py:345
  40.6 0.0 copy-done.9
  40.6 0.1 select_reduce_fusion
  40.7 0.0 copy-done.7
  40.7 0.0 copy-done.8
  40.7 0.0 copy-done.10
  40.8 0.0 copy-done.11
  40.8 0.1 copy.14
  40.9 0.1 eq.88
  41.1 0.0 copy-start.4
  41.1 25.2 %all-to-all-done.got = f32[16,27,8,128]{3,2,1,0:T(8,128)S(1)} async-done(((f32[16,27,8,128]{3,2,1,0:T(8,128)}), f32[16,27,8,128]{3,2,1,0:T(8,128)S(1)}, u32[]{:S(2)}, u32[]{:S(2)}) %all-to-all-start) | async-done | bytes 1769504 | tf_op jit(solution)/shard_map/all_to_all | solution.py:345
  66.3 0.8 plane_sum.1
  67.0 8.2 %all-to-all-start.1 = ((f32[8,32,128]{2,1,0:T(8,128)}), f32[8,32,128]{2,1,0:T(8,128)S(1)}, u32[]{:S(2)}, u32[]{:S(2)}) async-start(f32[8,32,128]{2,1,0:T(8,128)} %plane_sum.1), calls=%async_computation.1 | async-start | bytes 262144 | tf_op jit(solution)/shard_map/all_to_all | solution.py:347
  75.2 0.2 compare_convert_fusion.picks
  75.4 7.8 %all-to-all-done.1.got = f32[8,32,128]{2,1,0:T(8,128)S(1)} async-done(((f32[8,32,128]{2,1,0:T(8,128)}), f32[8,32,128]{2,1,0:T(8,128)S(1)}, u32[]{:S(2)}, u32[]{:S(2)}) %all-to-all-start.1) | async-done | bytes 131104 | tf_op jit(solution)/shard_map/all_to_all | solution.py:347
  83.2 1.0 spread_rows.1
  84.2 8.1 %all-to-all-start.2 = ((f32[256,4,128]{2,1,0:T(4,128)}), f32[256,4,128]{2,1,0:T(4,128)S(1)}, u32[]{:S(2)}, u32[]{:S(2)}) async-start(f32[256,4,128]{2,1,0:T(4,128)} %bitcast.10), calls=%async_computation.2 | async-start | bytes 1048576 | tf_op jit(solution)/shard_map/all_to_all | solution.py:349
  93.0 0.8 stack.64.meta
  93.8 19.9 %all-to-all-done.2 = f32[256,4,128]{2,1,0:T(4,128)S(1)} async-done(((f32[256,4,128]{2,1,0:T(4,128)}), f32[256,4,128]{2,1,0:T(4,128)S(1)}, u32[]{:S(2)}, u32[]{:S(2)}) %all-to-all-start.2) | async-done | bytes 524320 | tf_op jit(solution)/shard_map/all_to_all | solution.py:349
  113.7 0.0 copy-done.4
  113.7 5.3 %invert_apply.1 = (f32[640,256]{1,0:T(8,128)}, f32[1,128,128]{2,1,0:T(8,128)}) custom-call(s32[7]{0:T(128)S(1)} %stack.64.meta, f32[1024,128]{1,0:T(8,128)S(1)} %bitcast.14, f32[1]{0:T(128)} %bitcast.13.damping, f32[640,256]{1,0:T(8,128)S(1)} %copy-done.4), custom_call_target="tpu_custom_call" | custom-call | tf_op jit(solution)/shard_map/invert_apply/pallas_call | solution.py:292
  (4 shorter events, 0.0 us)
Async XLA Ops:
  3.7 2.2 %copy-start = (bf16[256,8192]{1,0:T(8,128)(2,1)S(1)}, bf16[256,8192]{1,0:T(8,128)(2,1)}, u32[]{:S(2)}) copy-start(bf16[256,8192]{1,0:T(8,128)(2,1)} %outgrads.3) | copy-start | bytes 12582916
  5.8 1.7 %copy-start.2 = (bf16[256,5120]{1,0:T(8,128)(2,1)S(1)}, bf16[256,5120]{1,0:T(8,128)(2,1)}, u32[]{:S(2)}) copy-start(bf16[256,5120]{1,0:T(8,128)(2,1)} %acts.3) | copy-start | bytes 7864324
  7.6 0.8 copy-start.5
  8.4 14.5 %copy-start.3 = (bf16[256,5120]{1,0:T(8,128)(2,1)S(1)}, bf16[256,5120]{1,0:T(8,128)(2,1)}, u32[]{:S(2)}) copy-start(bf16[256,5120]{1,0:T(8,128)(2,1)} %acts.3) | copy-start | bytes 7864324
  8.4 14.5 %copy-start.6 = (f32[1,128,128]{2,1,0:T(8,128)S(1)}, f32[1,128,128]{2,1,0:T(8,128)}, u32[]{:S(2)}) copy-start(f32[1,128,128]{2,1,0:T(8,128)} %prev.3) | copy-start | bytes 196612
  18.9 13.7 %collective-permute-start = (f32[16,27,8,128]{3,2,1,0:T(8,128)}, f32[16,27,8,128]{3,2,1,0:T(8,128)}, u32[]{:S(2)}, u32[]{:S(2)}) collective-permute-start(f32[16,27,8,128]{3,2,1,0:T(8,128)} %get-tuple-element.5), channel_id=1, source_target_pairs={{0,1},{1,0},{2,3},{3,2},{4,5},{5,4},{6,7},{7,6},{8,9},{9,8},{10,11... | collective-permute-start | bytes 5308424 | tf_op jit(solution)/shard_map/ppermute | solution.py:342
  23.0 2.2 %copy-start.1 = (bf16[256,8192]{1,0:T(8,128)(2,1)S(1)}, bf16[256,8192]{1,0:T(8,128)(2,1)}, u32[]{:S(2)}) copy-start(bf16[256,8192]{1,0:T(8,128)(2,1)} %outgrads.3) | copy-start | bytes 12582916
  35.4 5.2 %copy-start.9 = (s32[256]{0:T(256)S(1)}, s32[256]{0:T(256)}, u32[]{:S(2)}) copy-start(s32[256]{0:T(256)} %constant.185.clone) | copy-start | bytes 3076
  35.4 5.3 %copy-start.7 = (s32[256]{0:T(256)S(1)}, s32[256]{0:T(256)}, u32[]{:S(2)}) copy-start(s32[256]{0:T(256)} %constant.183.clone) | copy-start | bytes 3076
  35.4 5.3 %copy-start.8 = (s32[256]{0:T(256)S(1)}, s32[256]{0:T(256)}, u32[]{:S(2)}) copy-start(s32[256]{0:T(256)} %constant.184.clone) | copy-start | bytes 3076
  35.4 5.4 %copy-start.10 = (s32[256,1]{0,1:T(1,128)S(1)}, s32[256,1]{0,1:T(1,128)}, u32[]{:S(2)}) copy-start(s32[256,1]{0,1:T(1,128)} %constant.189) | copy-start | bytes 3076
  35.4 5.4 %copy-start.11 = (s32[256,1]{0,1:T(1,128)S(1)}, s32[256,1]{0,1:T(1,128)}, u32[]{:S(2)}) copy-start(s32[256,1]{0,1:T(1,128)} %constant.190) | copy-start | bytes 3076
  35.4 30.9 %all-to-all-start = ((f32[16,27,8,128]{3,2,1,0:T(8,128)}), f32[16,27,8,128]{3,2,1,0:T(8,128)S(1)}, u32[]{:S(2)}, u32[]{:S(2)}) async-start(f32[16,27,8,128]{3,2,1,0:T(8,128)} %add.180), calls=%async_computation | async-start | bytes 3538944 | tf_op jit(solution)/shard_map/all_to_all | solution.py:345
  41.1 72.6 %copy-start.4 = (f32[640,256]{1,0:T(8,128)S(1)}, f32[640,256]{1,0:T(8,128)}, u32[]{:S(2)}) copy-start(f32[640,256]{1,0:T(8,128)} %weight.1) | copy-start | bytes 1966084
  67.0 16.2 %all-to-all-start.1 = ((f32[8,32,128]{2,1,0:T(8,128)}), f32[8,32,128]{2,1,0:T(8,128)S(1)}, u32[]{:S(2)}, u32[]{:S(2)}) async-start(f32[8,32,128]{2,1,0:T(8,128)} %plane_sum.1), calls=%async_computation.1 | async-start | bytes 262144 | tf_op jit(solution)/shard_map/all_to_all | solution.py:347
  84.2 29.4 %all-to-all-start.2 = ((f32[256,4,128]{2,1,0:T(4,128)}), f32[256,4,128]{2,1,0:T(4,128)S(1)}, u32[]{:S(2)}, u32[]{:S(2)}) async-start(f32[256,4,128]{2,1,0:T(4,128)} %bitcast.10), calls=%async_computation.2 | async-start | bytes 1048576 | tf_op jit(solution)/shard_map/all_to_all | solution.py:349

commit v2 on v1

--- a/solution.py
+++ b/solution.py
@@ -60,102 +60,159 @@
     return lax.dot_general(x, x, (((0,), (0,)), ((), ())), preferred_element_type=jnp.float32)
 
 
-def partial_kernel(own, meta, acts, outgrads, prev, diag_in, out, diag_out, buf, odd, rows, sems, odd_sems):
-    half = meta[0]
+GROUPS = (12, 14)
+
+
+def partial_kernel(core_of, me_of, own, *refs):
+    if own:
+        acts, outgrads, prev_hbm, owner_hbm, diag_in, out, buf, prev, owner, sems, small_sems = refs
+    else:
+        acts, outgrads, prev_hbm, owner_hbm, out_hbm, diag_out = refs[:6]
+        buf, prev, owner, sems, small_sems, out, out_sems, odd, rows, odd_sems = refs[6:]
+    core, me = core_of(), me_of()
+    half = core if own else 1 - core
+    small = [
+        pltpu.make_async_copy(owner_hbm, owner, small_sems.at[0]),
+        pltpu.make_async_copy(prev_hbm, prev, small_sems.at[1]),
+    ]
+    small[0].start()
     copies, odd_copies = [], []
     for place in range(HALF):
         which, pair = pair_column(place, half)
-        src = outgrads if which else acts
         off = pl.multiple_of(pair * (2 * N), 2 * N)
-        copies.append(pltpu.make_async_copy(src.at[:, pl.ds(off, 2 * N)], buf.at[place], sems.at[place]))
+        src = (outgrads if which else acts).at[:, pl.ds(off, 2 * N)]
+        copies.append(pltpu.make_async_copy(src, buf.at[place], sems.at[place]))
         copies[-1].start()
+    small[1].start()
+    r, c = lower_mask()
     if not own:
         for place in range(HALF):
-            which, pair = pair_column(place, 1 - half)
-            src = outgrads if which else acts
+            which, pair = pair_column(place, core)
             off = pl.multiple_of(pair * (2 * N) + N, N)
-            odd_copies.append(
-                pltpu.make_async_copy(src.at[:, pl.ds(off, N)], odd.at[place], odd_sems.at[place])
-            )
+            src = (outgrads if which else acts).at[:, pl.ds(off, N)]
+            odd_copies.append(pltpu.make_async_copy(src, odd.at[place], odd_sems.at[place]))
             odd_copies[-1].start()
         rows[...] = jnp.zeros((N, N), jnp.float32)
-    r, c = lower_mask()
-    for place in range(HALF):
-        copies[place].wait()
-        first = gram(buf[place, :, :N])
-        second = gram(buf[place, :, N:])
-        packed = jnp.where(r <= c, first, second) * SCALE
-        out[:, place] = packed.reshape(16, 8, N)
+
+    small[0].wait()
+    block = jnp.int32(0)
+    for i in range(NB):
+        block = jnp.where(owner[i] == me, i + 1, block)
+    slot = jnp.maximum(block - 1, 0)
+    slot_half, slot_place = pair_home(slot)
+    second_of = slot % 2
+
+    done, sent = 0, []
+    for number, count in enumerate(GROUPS):
+        begin, end = done, done + count
+        done = end
+        for place in range(begin, end):
+            copies[place].wait()
+        for place in range(begin, end):
+            first = gram(buf[place, :, :N])
+            second = gram(buf[place, :, N:])
+            packed = jnp.where(r <= c, first, second) * SCALE
+            out[:, place] = packed.reshape(16, 8, N)
+            if not own:
+                line = jnp.sum(jnp.where(r == c, second, 0.0), axis=0, keepdims=True)
+                rows[pl.ds(32 * half + place, 1), :] = line * SCALE
+        if number == 0:
+            small[1].wait()
+
+        @pl.when((block > 0) & (slot_half == half) & (slot_place >= begin) & (slot_place < end))
+        def _():
+            mine = jnp.where((r > c) == (second_of == 1), prev[0] * ema_decay, 0.0)
+            out[:, slot_place] += mine.reshape(16, 8, N)
+
         if not own:
-            line = jnp.sum(jnp.where(r == c, second, 0.0), axis=0, keepdims=True)
-            rows[pl.ds(32 * half + place, 1), :] = line * SCALE
-    if not own:
-        for place in range(HALF):
-            odd_copies[place].wait()
-            x = odd[place].astype(jnp.float32)
-            rows[pl.ds(32 * (1 - half) + place, 1), :] = jnp.sum(x * x, axis=0, keepdims=True) * SCALE
-
-    block, slot_half, place, second_of = meta[1], meta[2], meta[3], meta[4]
-
-    @pl.when((block > 0) & (slot_half == half))
-    def _():
-        mine = jnp.where((r > c) == (second_of == 1), prev[0] * ema_decay, 0.0)
-        out[:, place] += mine.reshape(16, 8, N)
-
+            at = pl.ds(begin, count)
+            sent.append(pltpu.make_async_copy(out.at[:, at], out_hbm.at[:, at], out_sems.at[number]))
+            sent[-1].start()
     if own:
         out[:, HALF] = diag_in[...]
-    else:
-
-        @pl.when((block > 0) & (second_of == 1))
-        def _():
-            line = jnp.sum(jnp.where(r == c, prev[0], 0.0), axis=0, keepdims=True)
-            rows[pl.ds(32 * slot_half + place, 1), :] += line * ema_decay
-
-        diag = rows[...].T.reshape(16, 8, N)
-        diag_out[...] = diag
-        out[:, HALF] = diag
-
-
-def partials(meta, acts, outgrads, prev, diag=None):
+        return
+    for place in range(HALF):
+        odd_copies[place].wait()
+    for place in range(HALF):
+        x = odd[place].astype(jnp.float32)
+        rows[pl.ds(32 * core + place, 1), :] = jnp.sum(x * x, axis=0, keepdims=True) * SCALE
+
+    @pl.when((block > 0) & (second_of == 1))
+    def _():
+        line = jnp.sum(jnp.where(r == c, prev[0], 0.0), axis=0, keepdims=True)
+        rows[pl.ds(32 * slot_half + slot_place, 1), :] += line * ema_decay
+
+    diag = rows[...].T.reshape(16, 8, N)
+    diag_out[...] = diag
+    out[:, HALF] = diag
+    at = pl.ds(HALF, 1)
+    sent.append(pltpu.make_async_copy(out.at[:, at], out_hbm.at[:, at], out_sems.at[len(GROUPS)]))
+    sent[-1].start()
+    for copy in sent:
+        copy.wait()
+
+
+def partials(acts, outgrads, prev, owner, core_of, me_of, diag=None):
     own = diag is not None
     shape = jax.ShapeDtypeStruct((16, TILES, 8, N), jnp.float32)
     diag_shape = jax.ShapeDtypeStruct((16, 8, N), jnp.float32)
-    vmem = pl.BlockSpec(memory_space=pltpu.VMEM)
-    hbm = pl.BlockSpec(memory_space=pl.ANY)
-    scratch = [pltpu.VMEM((HALF, 256, 2 * N), jnp.bfloat16)]
-    if own:
-
-        def kernel(meta, acts, outgrads, prev, diag_in, out, buf, sems):
-            partial_kernel(True, meta, acts, outgrads, prev, diag_in, out, None, buf, None, None, sems, None)
-
-        scratch += [pltpu.SemaphoreType.DMA((HALF,))]
-    else:
-
-        def kernel(meta, acts, outgrads, prev, out, diag_out, buf, odd, rows, sems, odd_sems):
-            partial_kernel(
-                False, meta, acts, outgrads, prev, None, out, diag_out, buf, odd, rows, sems, odd_sems
-            )
-
+    hbm, vmem = pl.BlockSpec(memory_space=pltpu.HBM), pl.BlockSpec(memory_space=pltpu.VMEM)
+    scratch = [
+        pltpu.VMEM((HALF, 256, 2 * N), jnp.bfloat16),
+        pltpu.VMEM((1, N, N), jnp.float32),
+        pltpu.SMEM((SLOTS,), jnp.int32),
+        pltpu.SemaphoreType.DMA((HALF,)),
+        pltpu.SemaphoreType.DMA((2,)),
+    ]
+    if not own:
         scratch += [
+            pltpu.VMEM((16, TILES, 8, N), jnp.float32),
+            pltpu.SemaphoreType.DMA((len(GROUPS) + 1,)),
             pltpu.VMEM((HALF, 256, N), jnp.bfloat16),
             pltpu.VMEM((N, N), jnp.float32),
             pltpu.SemaphoreType.DMA((HALF,)),
-            pltpu.SemaphoreType.DMA((HALF,)),
         ]
     return pl.pallas_call(
-        kernel,
+        functools.partial(partial_kernel, core_of, me_of, own),
         out_shape=shape if own else (shape, diag_shape),
-        in_specs=[pl.BlockSpec(memory_space=pltpu.SMEM), hbm, hbm, vmem] + ([vmem] if own else []),
-        out_specs=vmem if own else (vmem, vmem),
+        in_specs=[hbm] * 4 + ([vmem] if own else []),
+        out_specs=vmem if own else (hbm, vmem),
         scratch_shapes=scratch,
-        compiler_params=pltpu.CompilerParams(vmem_limit_bytes=40 * 2**20),
+        compiler_params=pltpu.CompilerParams(vmem_limit_bytes=(50 if own else 61) * 2**20),
         name="own_half" if own else "other_half",
-    )(*((meta, acts, outgrads, prev) + ((diag,) if own else ())))
+    )(*((acts, outgrads, prev, owner) + ((diag,) if own else ())))
+
+
+CHUNKS = 4
+
+
+def add_kernel(own, received, out_hbm, out, sems):
+    copies = []
+    for i in range(CHUNKS):
+        at = pl.ds(i * (16 // CHUNKS), 16 // CHUNKS)
+        out[at] = own[at] + received[at]
+        copies.append(pltpu.make_async_copy(out.at[at], out_hbm.at[at], sems.at[i]))
+        copies[-1].start()
+    for copy in copies:
+        copy.wait()
+
+
+def add_cores(own, received):
+    hbm, vmem = pl.BlockSpec(memory_space=pltpu.HBM), pl.BlockSpec(memory_space=pltpu.VMEM)
+    return pl.pallas_call(
+        add_kernel,
+        out_shape=jax.ShapeDtypeStruct(own.shape, jnp.float32),
+        in_specs=[vmem, vmem],
+        out_specs=hbm,
+        scratch_shapes=[pltpu.VMEM(own.shape, jnp.float32), pltpu.SemaphoreType.DMA((CHUNKS,))],
+        compiler_params=pltpu.CompilerParams(vmem_limit_bytes=16 * 2**20),
+        name="add_cores",
+    )(own, received)
 
 
 def plane_kernel(got, out, total):
     for tile in range(TILES):
-        parts = [got[s, tile] for s in range(16)]
+        parts = [got[s, pl.ds(8 * tile, 8), :] for s in range(16)]
         while len(parts) > 1:
             parts = [a + b for a, b in zip(parts[::2], parts[1::2])]
         total[pl.ds(8 * tile, 8), :] = parts[0]
@@ -324,25 +381,27 @@
 
 
 def on_device(acts, outgrads, weight_grad, prev_factor, damping, owner):
-    core = lax.axis_index("c").astype(jnp.int32)
-    row = lax.axis_index(("zh", "x")).astype(jnp.int32)
-    col = lax.axis_index(("zl", "y", "c")).astype(jnp.int32)
-    me = row * 32 + col
+    core_of = lambda: lax.axis_index("c").astype(jnp.int32)
+    row_of = lambda: lax.axis_index(("zh", "x")).astype(jnp.int32)
+    col_of = lambda: lax.axis_index(("zl", "y", "c")).astype(jnp.int32)
+    me_of = lambda: row_of() * 32 + col_of()
+
+    other, diag = partials(acts, outgrads, prev_factor, owner, core_of, me_of)
+    received = lax.ppermute(other, "c", [(0, 1), (1, 0)])
+    own = partials(acts, outgrads, prev_factor, owner, core_of, me_of, diag)
+    chip = add_cores(own, received)
+
+    owner, _ = lax.optimization_barrier((owner, other))
+    core, row, col, me = core_of(), row_of(), col_of(), me_of()
     numbers = jnp.arange(NB, dtype=jnp.int32)
     block = jnp.sum(jnp.where(owner[:NB] == me, numbers + 1, 0))
     slot_half, slot_place = pair_home(jnp.maximum(block - 1, 0))
     slot_second = jnp.maximum(block - 1, 0) % 2
     slot = [block, slot_half, slot_place, slot_second]
-    other_meta = jnp.stack([1 - core] + slot).astype(jnp.int32)
-    own_meta = jnp.stack([core] + slot).astype(jnp.int32)
     apply_meta = jnp.stack([core, row, col] + slot).astype(jnp.int32)
     picks = picked_rows(owner, core)
 
-    other, diag = partials(other_meta, acts, outgrads, prev_factor)
-    received = lax.ppermute(other, "c", [(0, 1), (1, 0)])
-    own = partials(own_meta, acts, outgrads, prev_factor, diag)
-    chip = own + received
-    got = lax.all_to_all(chip, PLANE, 0, 0, tiled=True)
+    got = lax.all_to_all(chip.reshape(16, 8 * TILES, N), PLANE, 0, 0, tiled=True)
     by_depth = plane_sum(got)
     got = lax.all_to_all(by_depth, DEPTH, 0, 0, tiled=True)
     sent = spread_rows(got, picks)

time: 119 us -> 99 us (0.83)
  Pallas kernels: 24.8 us -> 17 us
  local copies, waits for them, and re-layouts: 9.56 us -> 1.86 us
  other arithmetic: 4.63 us -> 1.06 us
  waiting for transfers between devices: 52.9 us -> 51.5 us
    pallas_call x2 -> x3, Pallas kernels: 17.8 us -> 9.97 us  [the longest x2 8.68 us: partials(): pl.pallas_call(functools.partial(partial_kernel, core_of, me_of, own), ou...]
    unnamed x24 -> x18, local copies, waits for them, and re-layouts: 6.99 us -> 0.89 us
    add x1 -> x0, other arithmetic: 2.86 us -> none  [on_device(): chip = own + received]
    another operation x2 -> x0, local copies, waits for them, and re-layouts: 1.54 us -> none  [the longest x1 0.77 us: on_device(): other_meta = jnp.stack([1 - core] + slot).astype(jnp.int32)]
  transfers between devices with their start and end apart: 4 -> 4, of which waited for: 3 -> 3; matrix products, arithmetic and copies ran while one was open for 2% -> 2% of each run, Pallas kernels for 6% -> 3%
where the time goes in v2:
time: 99 us; the launch traced here: 98.6 us
  waiting for transfers between devices  51.5 us (52%)
  starting transfers between devices  25 us (25%)
  Pallas kernels  17 us (17%)
  between operations  2.24 us (2%)
  local copies, waits for them, and re-layouts  1.86 us (2%)
  other arithmetic  1.06 us (1%)
    all_to_all x1, waiting for transfers between devices, on_device(): lax.all_to_all(chip.reshape(16, 8 * TILES, N), PLANE, 0, 0, tiled=True)  24.5 us
    all_to_all x1, waiting for transfers between devices, on_device(): got = lax.all_to_all(sent.reshape(SLOTS, 4, N), SPREAD, 0, 0, tiled=True)  19.2 us
    pallas_call x2, Pallas kernels, partials(): pl.pallas_call(functools.partial(partial_kernel, core_of, me_of, own), ou...  8.68 us
    all_to_all x1, starting transfers between devices, on_device(): got = lax.all_to_all(by_depth, DEPTH, 0, 0, tiled=True)  8.3 us
    all_to_all x1, starting transfers between devices, on_device(): got = lax.all_to_all(sent.reshape(SLOTS, 4, N), SPREAD, 0, 0, tiled=True)  8.16 us
    all_to_all x1, waiting for transfers between devices, on_device(): got = lax.all_to_all(by_depth, DEPTH, 0, 0, tiled=True)  7.82 us
    pallas_call x1, Pallas kernels, apply_all(): pl.pallas_call(apply_kernel, out_shape=(jax.ShapeDtypeStruct(weight.shape...  5.26 us
    all_to_all x1, starting transfers between devices, on_device(): lax.all_to_all(chip.reshape(16, 8 * TILES, N), PLANE, 0, 0, tiled=True)  5.17 us
  transfers between devices with their start and end apart: 4, of which 3 were waited for; matrix products, arithmetic and copies ran while one was open for 2% of the time, Pallas kernels for 3%

profile of v2, /device:TPU:1, one launch (start us, length us, event | category | flops | bytes accessed | tf_op | source)
XLA Modules:
  0.0 98.6 jit_solution(16687023197220482078)
XLA Ops:
  0.6 0.0 copy-start.3
  0.6 0.0 copy-start.1
  0.6 5.6 %other_half.1 = (f32[16,27,8,128]{3,2,1,0:T(8,128)}, f32[16,8,128]{2,1,0:T(8,128)}) custom-call(bf16[256,5120]{1,0:T(8,128)(2,1)} %refs_0_.3, bf16[256,8192]{1,0:T(8,128)(2,1)} %refs_1_.3, f32[1,128,128]{2,1,0:T(8,128)} %refs_2_.3, s32[256]{0:T(256)} %refs_3_.3), custom_call_target="tpu_custom_call" | custom-call | tf_op jit(solution)/shard_map/other_half/pallas_call | solution.py:175
  6.3 3.3 %collective-permute-start = (f32[16,27,8,128]{3,2,1,0:T(8,128)}, f32[16,27,8,128]{3,2,1,0:T(8,128)S(1)}, u32[]{:S(2)}, u32[]{:S(2)}) collective-permute-start(f32[16,27,8,128]{3,2,1,0:T(8,128)} %get-tuple-element.5), channel_id=1, source_target_pairs={{0,1},{1,0},{2,3},{3,2},{4,5},{5,4},{6,7},{7,6},{8,9},{9,8},{10,11... | collective-permute-start | bytes 5308424 | tf_op jit(solution)/shard_map/ppermute | solution.py:390
  9.6 0.0 copy-done.3
  9.6 0.0 copy-done.1
  9.6 0.0 copy-start.2
  9.6 0.8 copy-done.2
  10.5 3.1 %own_half.1.own = f32[16,27,8,128]{3,2,1,0:T(8,128)S(1)} custom-call(bf16[256,5120]{1,0:T(8,128)(2,1)} %refs_0_.3, bf16[256,8192]{1,0:T(8,128)(2,1)} %refs_1_.3, f32[1,128,128]{2,1,0:T(8,128)S(1)} %copy-done.1, s32[256]{0:T(256)S(1)} %copy-done.3, f32[16,8,128]{2,1,0:T(8,128)S(1)} %copy-done.2), custom_call_target="tpu_custom_call" | custom-call | tf_op jit(solution)/shard_map/own_half/pallas_call | solution.py:175
  13.5 0.0 collective-permute-done.received
  13.5 1.3 %add_cores.1 = f32[16,27,8,128]{3,2,1,0:T(8,128)} custom-call(f32[16,27,8,128]{3,2,1,0:T(8,128)S(1)} %own_half.1.own, f32[16,27,8,128]{3,2,1,0:T(8,128)S(1)} %collective-permute-done.received), custom_call_target="tpu_custom_call" | custom-call | tf_op jit(solution)/shard_map/add_cores/pallas_call | solution.py:202
  14.8 0.0 copy-start.6
  14.8 0.0 copy-start.4
  14.9 0.0 copy-start.5
  14.9 0.0 copy-start.7
  14.9 0.0 copy-start.8
  14.9 5.2 %all-to-all-start = ((f32[16,216,128]{2,1,0:T(8,128)}), f32[16,216,128]{2,1,0:T(8,128)S(1)}, u32[]{:S(2)}, u32[]{:S(2)}) async-start(f32[16,216,128]{2,1,0:T(8,128)} %bitcast.7), calls=%async_computation | async-start | bytes 3538944 | tf_op jit(solution)/shard_map/all_to_all | solution.py:404
  20.1 0.7 fusion.5
  20.8 0.0 copy-done.6
  20.8 0.1 select_reduce_fusion
  20.9 0.0 copy-done.4
  20.9 0.0 copy-done.5
  21.0 0.0 copy-done.7
  21.0 0.0 copy-done.8
  21.0 0.1 copy.14
  21.1 0.1 eq.88
  21.3 24.5 %all-to-all-done.got = f32[16,216,128]{2,1,0:T(8,128)S(1)} async-done(((f32[16,216,128]{2,1,0:T(8,128)}), f32[16,216,128]{2,1,0:T(8,128)S(1)}, u32[]{:S(2)}, u32[]{:S(2)}) %all-to-all-start) | async-done | bytes 1769504 | tf_op jit(solution)/shard_map/all_to_all | solution.py:404
  45.8 0.8 plane_sum.1
  46.6 0.0 copy-start
  46.6 8.3 %all-to-all-start.1 = ((f32[8,32,128]{2,1,0:T(8,128)}), f32[8,32,128]{2,1,0:T(8,128)S(1)}, u32[]{:S(2)}, u32[]{:S(2)}) async-start(f32[8,32,128]{2,1,0:T(8,128)} %plane_sum.1), calls=%async_computation.1 | async-start | bytes 262144 | tf_op jit(solution)/shard_map/all_to_all | solution.py:406
  54.9 0.2 compare_convert_fusion.picks
  55.1 7.8 %all-to-all-done.1.got = f32[8,32,128]{2,1,0:T(8,128)S(1)} async-done(((f32[8,32,128]{2,1,0:T(8,128)}), f32[8,32,128]{2,1,0:T(8,128)S(1)}, u32[]{:S(2)}, u32[]{:S(2)}) %all-to-all-start.1) | async-done | bytes 131104 | tf_op jit(solution)/shard_map/all_to_all | solution.py:406
  62.9 1.0 %spread_rows.1 = f32[1024,128]{1,0:T(8,128)} custom-call(f32[8,32,128]{2,1,0:T(8,128)S(1)} %all-to-all-done.1.got, bf16[1024,96]{1,0:T(8,128)(2,1)S(1)} %compare_convert_fusion.picks), custom_call_target="tpu_custom_call" | custom-call | tf_op jit(solution)/shard_map/spread_rows/pallas_call | solution.py:253
  63.9 8.2 %all-to-all-start.2 = ((f32[256,4,128]{2,1,0:T(4,128)}), f32[256,4,128]{2,1,0:T(4,128)S(1)}, u32[]{:S(2)}, u32[]{:S(2)}) async-start(f32[256,4,128]{2,1,0:T(4,128)} %bitcast.10), calls=%async_computation.2 | async-start | bytes 1048576 | tf_op jit(solution)/shard_map/all_to_all | solution.py:408
  73.5 0.7 stack.46.meta
  74.2 19.2 %all-to-all-done.2 = f32[256,4,128]{2,1,0:T(4,128)S(1)} async-done(((f32[256,4,128]{2,1,0:T(4,128)}), f32[256,4,128]{2,1,0:T(4,128)S(1)}, u32[]{:S(2)}, u32[]{:S(2)}) %all-to-all-start.2) | async-done | bytes 524320 | tf_op jit(solution)/shard_map/all_to_all | solution.py:408
  93.4 0.0 copy-done
  93.4 5.3 %invert_apply.1 = (f32[640,256]{1,0:T(8,128)}, f32[1,128,128]{2,1,0:T(8,128)}) custom-call(s32[7]{0:T(128)S(1)} %stack.46.meta, f32[1024,128]{1,0:T(8,128)S(1)} %bitcast.14, f32[1]{0:T(128)} %bitcast.13.damping, f32[640,256]{1,0:T(8,128)S(1)} %copy-done), custom_call_target="tpu_custom_call" | custom-call | tf_op jit(solution)/shard_map/invert_apply/pallas_call | solution.py:349
  (4 shorter events, 0.0 us)
Async XLA Ops:
  0.6 9.0 %copy-start.3 = (s32[256]{0:T(256)S(1)}, s32[256]{0:T(256)}, u32[]{:S(2)}) copy-start(s32[256]{0:T(256)} %refs_3_.3) | copy-start | bytes 3076
  0.6 9.0 %copy-start.1 = (f32[1,128,128]{2,1,0:T(8,128)S(1)}, f32[1,128,128]{2,1,0:T(8,128)}, u32[]{:S(2)}) copy-start(f32[1,128,128]{2,1,0:T(8,128)} %refs_2_.3) | copy-start | bytes 196612
  6.3 7.2 %collective-permute-start = (f32[16,27,8,128]{3,2,1,0:T(8,128)}, f32[16,27,8,128]{3,2,1,0:T(8,128)S(1)}, u32[]{:S(2)}, u32[]{:S(2)}) collective-permute-start(f32[16,27,8,128]{3,2,1,0:T(8,128)} %get-tuple-element.5), channel_id=1, source_target_pairs={{0,1},{1,0},{2,3},{3,2},{4,5},{5,4},{6,7},{7,6},{8,9},{9,8},{10,11... | collective-permute-start | bytes 5308424 | tf_op jit(solution)/shard_map/ppermute | solution.py:390
  9.6 0.8 copy-start.2
  14.8 6.0 %copy-start.6 = (s32[256]{0:T(256)S(1)}, s32[256]{0:T(256)}, u32[]{:S(2)}) copy-start(s32[256]{0:T(256)} %constant.185.clone) | copy-start | bytes 3076
  14.8 6.1 %copy-start.4 = (s32[256]{0:T(256)S(1)}, s32[256]{0:T(256)}, u32[]{:S(2)}) copy-start(s32[256]{0:T(256)} %constant.184.clone) | copy-start | bytes 3076
  14.9 6.1 %copy-start.5 = (s32[256]{0:T(256)S(1)}, s32[256]{0:T(256)}, u32[]{:S(2)}) copy-start(s32[256]{0:T(256)} %constant.183.clone) | copy-start | bytes 3076
  14.9 6.1 %copy-start.7 = (s32[256,1]{0,1:T(1,128)S(1)}, s32[256,1]{0,1:T(1,128)}, u32[]{:S(2)}) copy-start(s32[256,1]{0,1:T(1,128)} %constant.190) | copy-start | bytes 3076
  14.9 6.1 %copy-start.8 = (s32[256,1]{0,1:T(1,128)S(1)}, s32[256,1]{0,1:T(1,128)}, u32[]{:S(2)}) copy-start(s32[256,1]{0,1:T(1,128)} %constant.189) | copy-start | bytes 3076
  14.9 30.9 %all-to-all-start = ((f32[16,216,128]{2,1,0:T(8,128)}), f32[16,216,128]{2,1,0:T(8,128)S(1)}, u32[]{:S(2)}, u32[]{:S(2)}) async-start(f32[16,216,128]{2,1,0:T(8,128)} %bitcast.7), calls=%async_computation | async-start | bytes 3538944 | tf_op jit(solution)/shard_map/all_to_all | solution.py:404
  46.6 46.8 %copy-start = (f32[640,256]{1,0:T(8,128)S(1)}, f32[640,256]{1,0:T(8,128)}, u32[]{:S(2)}) copy-start(f32[640,256]{1,0:T(8,128)} %weight.1) | copy-start | bytes 1966084
  46.6 16.3 %all-to-all-start.1 = ((f32[8,32,128]{2,1,0:T(8,128)}), f32[8,32,128]{2,1,0:T(8,128)S(1)}, u32[]{:S(2)}, u32[]{:S(2)}) async-start(f32[8,32,128]{2,1,0:T(8,128)} %plane_sum.1), calls=%async_computation.1 | async-start | bytes 262144 | tf_op jit(solution)/shard_map/all_to_all | solution.py:406
  63.9 29.5 %all-to-all-start.2 = ((f32[256,4,128]{2,1,0:T(4,128)}), f32[256,4,128]{2,1,0:T(4,128)S(1)}, u32[]{:S(2)}, u32[]{:S(2)}) async-start(f32[256,4,128]{2,1,0:T(4,128)} %bitcast.10), calls=%async_computation.2 | async-start | bytes 1048576 | tf_op jit(solution)/shard_map/all_to_all | solution.py:408

commit v3 on v2

v3 whole, which is shorter than its diff:
```python
import functools

import jax
import jax.numpy as jnp
import numpy as np
from jax import lax
from jax.experimental import pallas as pl
from jax.experimental.pallas import tpu as pltpu
from jax.sharding import Mesh
from jax.sharding import PartitionSpec as P

D = 5120
H = 8192
N = 128
ITERS = 6
TOKENS = 65536
NA = D // N
NB = NA + H // N
SLOTS = 256

ema_decay = 0.8

HALF = 26
TILES = HALF + 1
ALL = ("zh", "x", "zl", "y", "c")
PLANE = ("x", "y")
DEPTH = ("zh", "zl")
CHIPS = ("x", "y", "zh", "zl")
ROWS = 6


def pair_home(block):
    group, at = block // 10, (block % 10) // 2
    col = (block - NA) // 2
    last = at == 2
    high = at > 2
    a_half = jnp.where(last, group % 2, jnp.where(high, at - 3, at))
    a_place = jnp.where(last, 8 + group // 2, jnp.where(high, group + 4, group))
    is_a = block < NA
    return jnp.where(is_a, a_half, col % 2), jnp.where(is_a, a_place, 10 + col // 2)


def pair_column(place, half):
    if place < 8:
        return 0, 5 * (place % 4) + (3 if place >= 4 else 0) + half
    if place < 10:
        return 0, 5 * (half + 2 * (place - 8)) + 2
    return 1, 2 * (place - 10) + half


def lower_mask():
    r = lax.broadcasted_iota(jnp.int32, (N, N), 0)
    c = lax.broadcasted_iota(jnp.int32, (N, N), 1)
    return r, c


SCALE = (1.0 - ema_decay) / TOKENS


def gram(x):
    return lax.dot_general(x, x, (((0,), (0,)), ((), ())), preferred_element_type=jnp.float32)


GROUPS = (12, 14)


def partial_kernel(core_of, me_of, own, *refs):
    if own:
        acts, outgrads, prev_hbm, owner_hbm, out, buf, prev, owner, rows, sems, small_sems = refs
    else:
        acts, outgrads, prev_hbm, owner_hbm, out_hbm, buf, prev, owner, rows, sems, small_sems, out, out_sems = refs
    core, me = core_of(), me_of()
    half = core if own else 1 - core
    small = [
        pltpu.make_async_copy(owner_hbm, owner, small_sems.at[0]),
        pltpu.make_async_copy(prev_hbm, prev, small_sems.at[1]),
    ]
    small[0].start()
    copies = []
    for place in range(HALF):
        which, pair = pair_column(place, half)
        off = pl.multiple_of(pair * (2 * N), 2 * N)
        src = (outgrads if which else acts).at[:, pl.ds(off, 2 * N)]
        copies.append(pltpu.make_async_copy(src, buf.at[place], sems.at[place]))
        copies[-1].start()
    small[1].start()
    r, c = lower_mask()
    rows[...] = jnp.zeros((N, N), jnp.float32)

    small[0].wait()
    block = jnp.int32(0)
    for i in range(NB):
        block = jnp.where(owner[i] == me, i + 1, block)
    slot = jnp.maximum(block - 1, 0)
    slot_half, slot_place = pair_home(slot)
    second_of = slot % 2

    done, sent = 0, []
    for number, count in enumerate(GROUPS):
        begin, end = done, done + count
        done = end
        for place in range(begin, end):
            copies[place].wait()
        for place in range(begin, end):
            first = gram(buf[place, :, :N])
            second = gram(buf[place, :, N:])
            packed = jnp.where(r <= c, first, second) * SCALE
            out[:, place] = packed.reshape(16, 8, N)
            line = jnp.sum(jnp.where(r == c, second, 0.0), axis=0, keepdims=True)
            rows[pl.ds(32 * half + place, 1), :] = line * SCALE
        if number == 0:
            small[1].wait()

        @pl.when((block > 0) & (slot_half == half) & (slot_place >= begin) & (slot_place < end))
        def _():
            mine = jnp.where((r > c) == (second_of == 1), prev[0] * ema_decay, 0.0)
            out[:, slot_place] += mine.reshape(16, 8, N)

        at = pl.ds(begin, count)
        if end == HALF:

            @pl.when((block > 0) & (slot_half == half) & (second_of == 1))
            def _():
                line = jnp.sum(jnp.where(r == c, prev[0], 0.0), axis=0, keepdims=True)
                rows[pl.ds(32 * half + slot_place, 1), :] += line * ema_decay

            out[:, HALF] = rows[...].T.reshape(16, 8, N)
            at = pl.ds(begin, count + 1)
        if not own:
            sent.append(pltpu.make_async_copy(out.at[:, at], out_hbm.at[:, at], out_sems.at[number]))
            sent[-1].start()
    for copy in sent:
        copy.wait()


def partials(acts, outgrads, prev, owner, core_of, me_of, own):
    hbm, vmem = pl.BlockSpec(memory_space=pltpu.HBM), pl.BlockSpec(memory_space=pltpu.VMEM)
    scratch = [
        pltpu.VMEM((HALF, 256, 2 * N), jnp.bfloat16),
        pltpu.VMEM((1, N, N), jnp.float32),
        pltpu.SMEM((SLOTS,), jnp.int32),
        pltpu.VMEM((N, N), jnp.float32),
        pltpu.SemaphoreType.DMA((HALF,)),
        pltpu.SemaphoreType.DMA((2,)),
    ]
    if not own:
        scratch += [
            pltpu.VMEM((16, TILES, 8, N), jnp.float32),
            pltpu.SemaphoreType.DMA((len(GROUPS),)),
        ]
    return pl.pallas_call(
        functools.partial(partial_kernel, core_of, me_of, own),
        out_shape=jax.ShapeDtypeStruct((16, TILES, 8, N), jnp.float32),
        in_specs=[hbm] * 4,
        out_specs=vmem if own else hbm,
        scratch_shapes=scratch,
        compiler_params=pltpu.CompilerParams(vmem_limit_bytes=(50 if own else 61) * 2**20),
        name="own_half" if own else "other_half",
    )(acts, outgrads, prev, owner)


CHUNKS = 4


def add_kernel(own, received, out_hbm, out, sems):
    copies = []
    for i in range(CHUNKS):
        at = pl.ds(i * (16 // CHUNKS), 16 // CHUNKS)
        out[at] = own[at] + received[at]
        copies.append(pltpu.make_async_copy(out.at[at], out_hbm.at[at], sems.at[i]))
        copies[-1].start()
    for copy in copies:
        copy.wait()


def add_cores(own, received):
    hbm, vmem = pl.BlockSpec(memory_space=pltpu.HBM), pl.BlockSpec(memory_space=pltpu.VMEM)
    return pl.pallas_call(
        add_kernel,
        out_shape=jax.ShapeDtypeStruct(own.shape, jnp.float32),
        in_specs=[vmem, vmem],
        out_specs=hbm,
        scratch_shapes=[pltpu.VMEM(own.shape, jnp.float32), pltpu.SemaphoreType.DMA((CHUNKS,))],
        compiler_params=pltpu.CompilerParams(vmem_limit_bytes=16 * 2**20),
        name="add_cores",
    )(own, received)


def plane_kernel(got, out, total):
    for tile in range(TILES):
        parts = [got[s, pl.ds(8 * tile, 8), :] for s in range(16)]
        while len(parts) > 1:
            parts = [a + b for a, b in zip(parts[::2], parts[1::2])]
        total[pl.ds(8 * tile, 8), :] = parts[0]
    total[pl.ds(8 * TILES, 40), :] = jnp.zeros((40, N), jnp.float32)
    for z in range(8):
        out[z] = total[pl.ds(z, 32, stride=8), :]


def plane_sum(got):
    return pl.pallas_call(
        plane_kernel,
        out_shape=jax.ShapeDtypeStruct((8, 32, N), jnp.float32),
        in_specs=[pl.BlockSpec(memory_space=pltpu.VMEM)],
        out_specs=pl.BlockSpec(memory_space=pltpu.VMEM),
        scratch_shapes=[pltpu.VMEM((256, N), jnp.float32)],
        compiler_params=pltpu.CompilerParams(vmem_limit_bytes=40 * 2**20),
        name="plane_sum",
    )(got)


def thirds(x):
    high = x.astype(jnp.bfloat16)
    rest = x - high.astype(jnp.float32)
    mid = rest.astype(jnp.bfloat16)
    low = (rest - mid.astype(jnp.float32)).astype(jnp.bfloat16)
    return high, mid, low


def spread_kernel(got, picks, out):
    total = got[0]
    for z in range(1, 8):
        total = total + got[z]
    stacked = jnp.concatenate(thirds(total), axis=0)
    out[...] = jnp.dot(picks[...], stacked, preferred_element_type=jnp.float32)


def spread_rows(got, picks):
    return pl.pallas_call(
        spread_kernel,
        out_shape=jax.ShapeDtypeStruct((ROWS * N, N), jnp.float32),
        in_specs=[pl.BlockSpec(memory_space=pltpu.VMEM)] * 2,
        out_specs=pl.BlockSpec(memory_space=pltpu.VMEM),
        compiler_params=pltpu.CompilerParams(vmem_limit_bytes=40 * 2**20),
        name="spread_rows",
    )(got, picks)


def left_form(a):
    a1, a2, a3 = thirds(a)
    return jnp.concatenate([a1, a2], axis=1), jnp.concatenate([a1, a3], axis=1)


def mul(left, b):
    b1, b2, b3 = thirds(b)
    wide = jnp.concatenate(
        [jnp.concatenate([b1, b2], axis=1), jnp.concatenate([b2, b1], axis=1)], axis=0
    )
    main = jnp.dot(left[0], wide, preferred_element_type=jnp.float32)
    small = jnp.dot(left[1], jnp.concatenate([b3, b1], axis=0), preferred_element_type=jnp.float32)
    return main[:, :N] + (main[:, N:] + small)


def unpacked(packed, second, diags, lane):
    r, c = lower_mask()
    lower, on = r > c, r == c
    flipped = packed.T
    if isinstance(second, int) and second == 0:
        return jnp.where(lower, flipped, packed)
    column = jnp.sum(jnp.where(c == lane, diags, 0.0), axis=1, keepdims=True)
    if isinstance(second, int):
        return jnp.where(on, column, jnp.where(lower, packed, flipped))
    straight = jnp.where(lower, second, 1 - second) == 1
    return jnp.where(on & (second == 1), column, jnp.where(straight, packed, flipped))


def inverses(blocks, damping):
    r, c = lower_mask()
    eye = jnp.where(r == c, 1.0, 0.0)
    damped, approx = [], []
    for one in blocks:
        one = one + damping * eye
        bound = jnp.max(jnp.sum(jnp.abs(one), axis=0, keepdims=True), axis=1, keepdims=True)
        start = 1.0 / bound
        damped.append(left_form(one))
        approx.append((2.0 * eye - one * start) * start)
    for _ in range(ITERS - 1):
        rest = [2.0 * eye - mul(d, x) for d, x in zip(damped, approx)]
        approx = [mul(left_form(x), y) for x, y in zip(approx, rest)]
    return approx


def both_sides(left, w, right):
    a12, a13 = left_form(left)
    a1 = a12[:, :N]
    w1, w2, w3 = thirds(w)
    main = jnp.dot(a12, jnp.concatenate([w1, w1], axis=0), preferred_element_type=jnp.float32)
    cross = jnp.dot(a12, jnp.concatenate([w2, w2], axis=0), preferred_element_type=jnp.float32)
    small = jnp.dot(
        jnp.concatenate([a1, a13[:, N:]], axis=1),
        jnp.concatenate([w3, w1], axis=0),
        preferred_element_type=jnp.float32,
    )
    product = main + (cross + small)
    return jnp.concatenate([mul(left_form(product[:, j * N : (j + 1) * N]), right[j]) for j in range(2)], axis=1)


def group_rows(index, odd_row):
    place = 4 * (1 - odd_row) if isinstance(index, str) else index + odd_row
    return pl.ds(pl.multiple_of(place * N, N), N)


def near_kernel(meta, own, damping, weight, rows_out, right_out):
    core, row, col = meta[0], meta[1], meta[2]
    group, odd_row = row // 2, row % 2

    def fetch(k):
        return own[pl.ds(k, N, stride=ROWS), :]

    diags, first, last = fetch(3), fetch(0), fetch(2)
    lane = 32 * core + group + 4 * odd_row
    blocks = [unpacked(first, second, diags, lane) for second in range(2)]
    blocks += [unpacked(last, second, diags, 32 * core + 10 + col // 2) for second in range(2)]
    approx = inverses(blocks, damping[0])
    for i in range(2):
        rows_out[pl.ds(i * N, N), :] = both_sides(approx[i], weight[group_rows(2 * core + i, odd_row), :], approx[2:])
        right_out[i] = approx[2 + i]


def far_kernel(meta, own, other, damping, weight, rows_in, right_in, out, updated):
    core, row = meta[0], meta[1]
    block, slot_half, slot_place, slot_second = meta[3], meta[4], meta[5], meta[6]
    group, odd_row = row // 2, row % 2
    fifth_half = group % 2

    def fetch(ref, k):
        return ref[pl.ds(k, N, stride=ROWS), :]

    diags = fetch(own, 3) + fetch(other, 3)
    first = fetch(other, 0)
    fifth = jnp.where(fifth_half == core, fetch(own, 1), fetch(other, 1))
    lane = 32 * (1 - core) + group + 4 * odd_row
    blocks = [unpacked(first, second, diags, lane) for second in range(2)]
    blocks.append(unpacked(fifth, odd_row, diags, 32 * fifth_half + 8 + group // 2))
    mine = jnp.where(slot_half == core, fetch(own, 4 + core), fetch(other, 4 + core))
    fresh = unpacked(mine, slot_second, diags, 32 * slot_half + slot_place)
    updated[0] = jnp.where(block > 0, fresh, 0.0)

    approx = inverses(blocks, damping[0])
    right = [right_in[0], right_in[1]]
    for i in range(2):
        out[group_rows(2 * core + i, odd_row), :] = rows_in[pl.ds(i * N, N), :]
        at = group_rows(2 * (1 - core) + i, odd_row)
        out[at, :] = both_sides(approx[i], weight[at, :], right)
    at = group_rows("fifth", odd_row)
    out[at, :] = both_sides(approx[2], weight[at, :], right)


def apply_near(meta, own, damping, weight):
    vmem, smem = pl.BlockSpec(memory_space=pltpu.VMEM), pl.BlockSpec(memory_space=pltpu.SMEM)
    return pl.pallas_call(
        near_kernel,
        out_shape=(
            jax.ShapeDtypeStruct((2 * N, 2 * N), jnp.float32),
            jax.ShapeDtypeStruct((2, N, N), jnp.float32),
        ),
        in_specs=[smem, vmem, smem, vmem],
        out_specs=(vmem, vmem),
        compiler_params=pltpu.CompilerParams(vmem_limit_bytes=40 * 2**20),
        name="apply_near",
    )(meta, own, damping, weight)


def apply_far(meta, own, other, damping, weight, rows, right):
    vmem, smem = pl.BlockSpec(memory_space=pltpu.VMEM), pl.BlockSpec(memory_space=pltpu.SMEM)
    return pl.pallas_call(
        far_kernel,
        out_shape=(
            jax.ShapeDtypeStruct(weight.shape, jnp.float32),
            jax.ShapeDtypeStruct((1, N, N), jnp.float32),
        ),
        in_specs=[smem, vmem, vmem, smem, vmem, vmem, vmem],
        out_specs=(vmem, vmem),
        compiler_params=pltpu.CompilerParams(vmem_limit_bytes=40 * 2**20),
        name="apply_far",
    )(meta, own, other, damping, weight, rows, right)


def picked_rows(owner, half):
    x, y, zh, zl = np.unravel_index(np.arange(N), (4, 4, 2, 4))
    row, pair_col = zh * 4 + x, zl * 4 + y
    group, odd_row = row // 2, row % 2
    fixed = [group + 4 * odd_row, 8 + group // 2, 10 + pair_col, np.full(N, HALF)]
    halves, places = pair_home(jnp.arange(NB, dtype=jnp.int32))
    slots = []
    for core in range(2):
        slot = jnp.asarray(row * 32 + pair_col * 2 + core, jnp.int32)
        matches = (owner[:NB, None] == slot[None, :]) & (halves == half)[:, None]
        slots.append(jnp.sum(jnp.where(matches, places[:, None], 0), axis=0))
    rows = jnp.stack([jnp.asarray(f) for f in fixed] + slots, axis=1).astype(jnp.int32)
    wanted = jnp.arange(96, dtype=jnp.int32) % 32
    return (rows[:, :, None] == wanted).astype(jnp.bfloat16).reshape(ROWS * N, 96)


def on_device(acts, outgrads, weight_grad, prev_factor, damping, owner):
    core_of = lambda: lax.axis_index("c").astype(jnp.int32)
    row_of = lambda: lax.axis_index(("zh", "x")).astype(jnp.int32)
    col_of = lambda: lax.axis_index(("zl", "y", "c")).astype(jnp.int32)
    me_of = lambda: row_of() * 32 + col_of()

    swap = [(0, 1), (1, 0)]
    other = partials(acts, outgrads, prev_factor, owner, core_of, me_of, False)
    received = lax.ppermute(other, "c", swap)
    own = partials(acts, outgrads, prev_factor, owner, core_of, me_of, True)
    chip = add_cores(own, received)

    owner, _ = lax.optimization_barrier((owner, other))
    core, row, col, me = core_of(), row_of(), col_of(), me_of()
    numbers = jnp.arange(NB, dtype=jnp.int32)
    block = jnp.sum(jnp.where(owner[:NB] == me, numbers + 1, 0))
    slot_half, slot_place = pair_home(jnp.maximum(block - 1, 0))
    slot_second = jnp.maximum(block - 1, 0) % 2
    slot = [block, slot_half, slot_place, slot_second]
    apply_meta = jnp.stack([core, row, col] + slot).astype(jnp.int32)
    picks = picked_rows(owner, core)

    got = lax.all_to_all(chip.reshape(16, 8 * TILES, N), PLANE, 0, 0, tiled=True)
    by_depth = plane_sum(got)
    got = lax.all_to_all(by_depth, DEPTH, 0, 0, tiled=True)
    damping = damping.reshape(1)
    got, apply_meta, damping = lax.optimization_barrier((got, apply_meta, damping))
    sent = spread_rows(got, picks)
    near = lax.all_to_all(sent.reshape(N, ROWS, 1, N), CHIPS, 0, 0, tiled=True).reshape(ROWS * N, N)
    far = lax.ppermute(near, "c", swap)
    rows, right = apply_near(apply_meta, near, damping, weight_grad)
    return apply_far(apply_meta, near, far, damping, weight_grad, rows, right)


def solution(mesh):
    fine = Mesh(mesh.devices.reshape(2, 4, 4, 4, 2), ALL)
    row, col = ("zh", "x"), ("zl", "y", "c")
    placed = (P(ALL, None), P(ALL, None), P(row, col), P(ALL, None, None), P(), P())
    return jax.shard_map(
        on_device,
        mesh=fine,
        in_specs=placed,
        out_specs=(P(row, col), P(ALL, None, None)),
        check_vma=False,
    )
```

time: 99 us -> 93.7 us (0.946)
  waiting for transfers between devices: 51.5 us -> 30.3 us
  blocking collectives: 0 us -> 19.7 us
  starting transfers between devices: 25 us -> 21.6 us
    all_to_all x0 -> x1, blocking collectives: none -> 19.7 us  [on_device(): lax.all_to_all(sent.reshape(N, ROWS, 1, N), CHIPS, 0, 0, tiled=True)]
    all_to_all x1 -> x0, waiting for transfers between devices: 19.2 us -> none  [on_device(): got = lax.all_to_all(sent.reshape(SLOTS, 4, N), SPREAD, 0, 0, tiled=True)]
    all_to_all x1 -> x0, starting transfers between devices: 8.16 us -> none  [on_device(): got = lax.all_to_all(sent.reshape(SLOTS, 4, N), SPREAD, 0, 0, tiled=True)]
    ppermute x1 -> x2, starting transfers between devices: 3.33 us -> 8.21 us  [the longest x1 4.89 us: on_device(): far = lax.ppermute(near, 'c', swap)]
    pallas_call x2 -> x3, Pallas kernels: 6.27 us -> 8 us  [the longest x1 4.5 us: apply_far(): pl.pallas_call(far_kernel, out_shape=(jax.ShapeDtypeStruct(weight.shape,...]
    all_to_all x1, waiting for transfers between devices: 24.5 us -> 22.9 us  [on_device(): lax.all_to_all(chip.reshape(16, 8 * TILES, N), PLANE, 0, 0, tiled=True)]
    pallas_call x2, Pallas kernels: 8.68 us -> 7.32 us  [partials(): pl.pallas_call(functools.partial(partial_kernel, core_of, me_of, own), ou...]
  transfers between devices with their start and end apart: 4 -> 4, of which waited for: 3 -> 3; matrix products, arithmetic and copies ran while one was open for 2% -> 2% of each run, Pallas kernels for 3% -> 7%
where the time goes in v3:
time: 93.7 us; the launch traced here: 93.3 us
  waiting for transfers between devices  30.3 us (32%)
  starting transfers between devices  21.6 us (23%)
  blocking collectives  19.7 us (21%)
  Pallas kernels  17.4 us (19%)
  between operations  2.29 us (2%)
  local copies, waits for them, and re-layouts  1.04 us (1%)
  other arithmetic  1.02 us (1%)
    all_to_all x1, waiting for transfers between devices, on_device(): lax.all_to_all(chip.reshape(16, 8 * TILES, N), PLANE, 0, 0, tiled=True)  22.9 us
    all_to_all x1, blocking collectives, on_device(): lax.all_to_all(sent.reshape(N, ROWS, 1, N), CHIPS, 0, 0, tiled=True)  19.7 us
    all_to_all x1, starting transfers between devices, on_device(): got = lax.all_to_all(by_depth, DEPTH, 0, 0, tiled=True)  8.2 us
    pallas_call x2, Pallas kernels, partials(): pl.pallas_call(functools.partial(partial_kernel, core_of, me_of, own), ou...  7.32 us
    all_to_all x1, waiting for transfers between devices, on_device(): got = lax.all_to_all(by_depth, DEPTH, 0, 0, tiled=True)  7.04 us
    all_to_all x1, starting transfers between devices, on_device(): lax.all_to_all(chip.reshape(16, 8 * TILES, N), PLANE, 0, 0, tiled=True)  5.16 us
    ppermute x1, starting transfers between devices, on_device(): far = lax.ppermute(near, 'c', swap)  4.89 us
    pallas_call x1, Pallas kernels, apply_far(): pl.pallas_call(far_kernel, out_shape=(jax.ShapeDtypeStruct(weight.shape,...  4.5 us
  transfers between devices with their start and end apart: 4, of which 3 were waited for; matrix products, arithmetic and copies ran while one was open for 2% of the time, Pallas kernels for 7%

profile of v3, /device:TPU:1, one launch (start us, length us, event | category | flops | bytes accessed | tf_op | source)
XLA Modules:
  0.0 93.3 jit_solution(7044963931800197053)
XLA Ops:
  0.6 0.0 copy-start.1
  0.6 0.0 copy-start.2
  0.6 4.2 %other_half.1 = f32[16,27,8,128]{3,2,1,0:T(8,128)} custom-call(bf16[256,5120]{1,0:T(8,128)(2,1)} %refs_0_.3, bf16[256,8192]{1,0:T(8,128)(2,1)} %refs_1_.3, f32[1,128,128]{2,1,0:T(8,128)} %refs_2_.3, s32[256]{0:T(256)} %refs_3_.3), custom_call_target="tpu_custom_call" | custom-call | tf_op jit(solution)/shard_map/other_half/pallas_call | solution.py:151
  4.8 3.3 %collective-permute-start = (f32[16,27,8,128]{3,2,1,0:T(8,128)}, f32[16,27,8,128]{3,2,1,0:T(8,128)S(1)}, u32[]{:S(2)}, u32[]{:S(2)}) collective-permute-start(f32[16,27,8,128]{3,2,1,0:T(8,128)} %other_half.1), channel_id=1, source_target_pairs={{0,1},{1,0},{2,3},{3,2},{4,5},{5,4},{6,7},{7,6},{8,9},{9,8},{10,11... | collective-permute-start | bytes 5308424 | tf_op jit(solution)/shard_map/ppermute | solution.py:403
  8.2 0.0 copy-done.1
  8.2 0.0 copy-done.2
  8.2 3.1 %own_half.1.own = f32[16,27,8,128]{3,2,1,0:T(8,128)S(1)} custom-call(bf16[256,5120]{1,0:T(8,128)(2,1)} %refs_0_.3, bf16[256,8192]{1,0:T(8,128)(2,1)} %refs_1_.3, f32[1,128,128]{2,1,0:T(8,128)S(1)} %copy-done.1, s32[256]{0:T(256)S(1)} %copy-done.2), custom_call_target="tpu_custom_call" | custom-call | tf_op jit(solution)/shard_map/own_half/pallas_call | solution.py:151
  11.3 0.4 collective-permute-done.received
  11.7 1.3 %add_cores.1 = f32[16,27,8,128]{3,2,1,0:T(8,128)} custom-call(f32[16,27,8,128]{3,2,1,0:T(8,128)S(1)} %own_half.1.own, f32[16,27,8,128]{3,2,1,0:T(8,128)S(1)} %collective-permute-done.received), custom_call_target="tpu_custom_call" | custom-call | tf_op jit(solution)/shard_map/add_cores/pallas_call | solution.py:178
  13.0 0.0 copy-start.6
  13.0 0.0 copy-start.7
  13.0 0.0 copy-start.3
  13.1 0.0 copy-start.4
  13.1 0.0 copy-start.5
  13.1 5.2 %all-to-all-start = ((f32[16,216,128]{2,1,0:T(8,128)}), f32[16,216,128]{2,1,0:T(8,128)S(1)}, u32[]{:S(2)}, u32[]{:S(2)}) async-start(f32[16,216,128]{2,1,0:T(8,128)} %bitcast), calls=%async_computation | async-start | bytes 3538944 | tf_op jit(solution)/shard_map/all_to_all | solution.py:417
  18.3 0.7 fusion.5
  19.8 0.0 copy-done.6
  19.8 0.0 copy-done.7
  19.8 0.1 select_reduce_fusion
  19.9 0.0 copy-done.3
  19.9 0.0 copy-done.4
  19.9 0.0 copy-done.5
  20.0 0.1 copy.17
  20.1 0.1 eq.97
  20.3 0.0 copy-start
  20.3 22.9 %all-to-all-done.got = f32[16,216,128]{2,1,0:T(8,128)S(1)} async-done(((f32[16,216,128]{2,1,0:T(8,128)}), f32[16,216,128]{2,1,0:T(8,128)S(1)}, u32[]{:S(2)}, u32[]{:S(2)}) %all-to-all-start) | async-done | bytes 1769504 | tf_op jit(solution)/shard_map/all_to_all | solution.py:417
  43.2 0.8 plane_sum.1
  44.0 8.2 %all-to-all-start.1 = ((f32[8,32,128]{2,1,0:T(8,128)}), f32[8,32,128]{2,1,0:T(8,128)S(1)}, u32[]{:S(2)}, u32[]{:S(2)}) async-start(f32[8,32,128]{2,1,0:T(8,128)} %plane_sum.1), calls=%async_computation.1 | async-start | bytes 262144 | tf_op jit(solution)/shard_map/all_to_all | solution.py:419
  52.1 0.7 stack.52.meta
  52.9 0.2 compare_convert_fusion.picks
  53.0 7.0 %all-to-all-done.1.got = f32[8,32,128]{2,1,0:T(8,128)S(1)} async-done(((f32[8,32,128]{2,1,0:T(8,128)}), f32[8,32,128]{2,1,0:T(8,128)S(1)}, u32[]{:S(2)}, u32[]{:S(2)}) %all-to-all-start.1) | async-done | bytes 131104 | tf_op jit(solution)/shard_map/all_to_all | solution.py:419
  60.1 0.2 spread_rows.1
  60.3 19.7 %all_to_all.15 = f32[128,6,1,128]{3,2,1,0:T(1,128)S(1)} all-to-all(f32[128,6,1,128]{3,2,1,0:T(1,128)S(1)} %bitcast.18), channel_id=1, replica_groups=mesh['zh'=2,'x'=4,'zl'=4,'y'=4,'c'=2] {'x','y','zh','zl'}, dimensions={0} | all-to-all | bytes 786432 | tf_op jit(solution)/shard_map/all_to_all | solution.py:423
  80.0 4.9 %collective-permute-start.1 = (f32[768,128]{1,0:T(8,128)S(1)}, f32[768,128]{1,0:T(8,128)S(1)}, u32[]{:S(2)}, u32[]{:S(2)}) collective-permute-start(f32[768,128]{1,0:T(8,128)S(1)} %bitcast.15), channel_id=1, source_target_pairs={{0,1},{1,0},{2,3},{3,2},{4,5},{5,4},{6,7},{7,6},{8,9},{9,8},{10,11... | collective-permute-start | bytes 1179656 | tf_op jit(solution)/shard_map/ppermute | solution.py:424
  85.5 0.0 copy-done
  85.5 3.3 %apply_near.1 = (f32[256,256]{1,0:T(8,128)S(1)}, f32[2,128,128]{2,1,0:T(8,128)S(1)}) custom-call(s32[7]{0:T(128)S(1)} %stack.52.meta, f32[768,128]{1,0:T(8,128)S(1)} %bitcast.16, f32[1]{0:T(128)} %bitcast.13.damping, f32[640,256]{1,0:T(8,128)S(1)} %copy-done), custom_call_target="tpu_custom_call" | custom-call | tf_op jit(solution)/shard_map/apply_near/pallas_call | solution.py:351
  88.8 0.0 collective-permute-done.1.other
  88.8 4.5 %apply_far.1 = (f32[640,256]{1,0:T(8,128)}, f32[1,128,128]{2,1,0:T(8,128)}) custom-call(s32[7]{0:T(128)S(1)} %stack.52.meta, f32[768,128]{1,0:T(8,128)S(1)} %bitcast.17, f32[768,128]{1,0:T(8,128)S(1)} %collective-permute-done.1.other, f32[1]{0:T(128)} %bitcast.14.damping, f32[640,256]{1,0:T(8,128)S(1)} %copy-done, f32[256,256]{1,0:T(8,128)S(1)} %get-tuple-element.12.rows_in, ...), custom_call_target="tpu_custom_call" | custom-call | tf_op jit(solution)/shard_map/apply_far/pallas_call | solution.py:366
  (4 shorter events, 0.1 us)
Async XLA Ops:
  0.6 7.5 %copy-start.1 = (f32[1,128,128]{2,1,0:T(8,128)S(1)}, f32[1,128,128]{2,1,0:T(8,128)}, u32[]{:S(2)}) copy-start(f32[1,128,128]{2,1,0:T(8,128)} %refs_2_.3) | copy-start | bytes 196612
  0.6 7.5 %copy-start.2 = (s32[256]{0:T(256)S(1)}, s32[256]{0:T(256)}, u32[]{:S(2)}) copy-start(s32[256]{0:T(256)} %refs_3_.3) | copy-start | bytes 3076
  4.8 6.9 %collective-permute-start = (f32[16,27,8,128]{3,2,1,0:T(8,128)}, f32[16,27,8,128]{3,2,1,0:T(8,128)S(1)}, u32[]{:S(2)}, u32[]{:S(2)}) collective-permute-start(f32[16,27,8,128]{3,2,1,0:T(8,128)} %other_half.1), channel_id=1, source_target_pairs={{0,1},{1,0},{2,3},{3,2},{4,5},{5,4},{6,7},{7,6},{8,9},{9,8},{10,11... | collective-permute-start | bytes 5308424 | tf_op jit(solution)/shard_map/ppermute | solution.py:403
  13.0 6.7 %copy-start.6 = (s32[128]{0:T(128)S(1)}, s32[128]{0:T(128)}, u32[]{:S(2)}) copy-start(s32[128]{0:T(128)} %constant.183.clone) | copy-start | bytes 1540
  13.0 6.7 %copy-start.7 = (s32[128]{0:T(128)S(1)}, s32[128]{0:T(128)}, u32[]{:S(2)}) copy-start(s32[128]{0:T(128)} %constant.184.clone) | copy-start | bytes 1540
  13.0 6.9 %copy-start.3 = (s32[128,1]{0,1:T(1,128)S(1)}, s32[128,1]{0,1:T(1,128)}, u32[]{:S(2)}) copy-start(s32[128,1]{0,1:T(1,128)} %constant.190) | copy-start | bytes 1540
  13.1 6.9 %copy-start.4 = (s32[128,1]{0,1:T(1,128)S(1)}, s32[128,1]{0,1:T(1,128)}, u32[]{:S(2)}) copy-start(s32[128,1]{0,1:T(1,128)} %constant.191) | copy-start | bytes 1540
  13.1 6.9 %copy-start.5 = (s32[128,1]{0,1:T(1,128)S(1)}, s32[128,1]{0,1:T(1,128)}, u32[]{:S(2)}) copy-start(s32[128,1]{0,1:T(1,128)} %constant.192) | copy-start | bytes 1540
  13.1 30.1 %all-to-all-start = ((f32[16,216,128]{2,1,0:T(8,128)}), f32[16,216,128]{2,1,0:T(8,128)S(1)}, u32[]{:S(2)}, u32[]{:S(2)}) async-start(f32[16,216,128]{2,1,0:T(8,128)} %bitcast), calls=%async_computation | async-start | bytes 3538944 | tf_op jit(solution)/shard_map/all_to_all | solution.py:417
  20.3 65.2 %copy-start = (f32[640,256]{1,0:T(8,128)S(1)}, f32[640,256]{1,0:T(8,128)}, u32[]{:S(2)}) copy-start(f32[640,256]{1,0:T(8,128)} %weight.3) | copy-start | bytes 1966084
  44.0 16.1 %all-to-all-start.1 = ((f32[8,32,128]{2,1,0:T(8,128)}), f32[8,32,128]{2,1,0:T(8,128)S(1)}, u32[]{:S(2)}, u32[]{:S(2)}) async-start(f32[8,32,128]{2,1,0:T(8,128)} %plane_sum.1), calls=%async_computation.1 | async-start | bytes 262144 | tf_op jit(solution)/shard_map/all_to_all | solution.py:419
  80.0 8.9 %collective-permute-start.1 = (f32[768,128]{1,0:T(8,128)S(1)}, f32[768,128]{1,0:T(8,128)S(1)}, u32[]{:S(2)}, u32[]{:S(2)}) collective-permute-start(f32[768,128]{1,0:T(8,128)S(1)} %bitcast.15), channel_id=1, source_target_pairs={{0,1},{1,0},{2,3},{3,2},{4,5},{5,4},{6,7},{7,6},{8,9},{9,8},{10,11... | collective-permute-start | bytes 1179656 | tf_op jit(solution)/shard_map/ppermute | solution.py:424

commit v4 on v3

--- a/solution.py
+++ b/solution.py
@@ -236,19 +236,40 @@
     )(got, picks)
 
 
+def halves(x):
+    high = x.astype(jnp.bfloat16)
+    return high, (x - high.astype(jnp.float32)).astype(jnp.bfloat16)
+
+
 def left_form(a):
-    a1, a2, a3 = thirds(a)
-    return jnp.concatenate([a1, a2], axis=1), jnp.concatenate([a1, a3], axis=1)
+    return jnp.concatenate(halves(a), axis=1)
+
+
+def right_form(b):
+    b1, b2 = halves(b)
+    return jnp.concatenate([jnp.concatenate([b1, b2], axis=1), jnp.concatenate([b2, b1], axis=1)], axis=0)
+
+
+def times(left, right):
+    four = jnp.dot(left, right, preferred_element_type=jnp.float32)
+    return four[:, :N] + four[:, N:]
 
 
 def mul(left, b):
-    b1, b2, b3 = thirds(b)
-    wide = jnp.concatenate(
-        [jnp.concatenate([b1, b2], axis=1), jnp.concatenate([b2, b1], axis=1)], axis=0
+    return times(left, right_form(b))
+
+
+def square(e):
+    e1 = e.astype(jnp.bfloat16)
+    low = e - e1.astype(jnp.float32)
+    e2 = low.astype(jnp.bfloat16)
+    e3 = (low - e2.astype(jnp.float32)).astype(jnp.bfloat16)
+    wide = jnp.concatenate([jnp.concatenate([e1, e2], axis=1), jnp.concatenate([e2, e1], axis=1)], axis=0)
+    four = jnp.dot(jnp.concatenate([e1, e2], axis=1), wide, preferred_element_type=jnp.float32)
+    two = jnp.dot(
+        jnp.concatenate([e1, e3], axis=1), jnp.concatenate([e3, e1], axis=0), preferred_element_type=jnp.float32
     )
-    main = jnp.dot(left[0], wide, preferred_element_type=jnp.float32)
-    small = jnp.dot(left[1], jnp.concatenate([b3, b1], axis=0), preferred_element_type=jnp.float32)
-    return main[:, :N] + (main[:, N:] + small)
+    return four[:, :N] + (four[:, N:] + two)
 
 
 def unpacked(packed, second, diags, lane):
@@ -267,32 +288,31 @@
 def inverses(blocks, damping):
     r, c = lower_mask()
     eye = jnp.where(r == c, 1.0, 0.0)
-    damped, approx = [], []
+    rest, approx = [], []
     for one in blocks:
         one = one + damping * eye
         bound = jnp.max(jnp.sum(jnp.abs(one), axis=0, keepdims=True), axis=1, keepdims=True)
         start = 1.0 / bound
-        damped.append(left_form(one))
-        approx.append((2.0 * eye - one * start) * start)
-    for _ in range(ITERS - 1):
-        rest = [2.0 * eye - mul(d, x) for d, x in zip(damped, approx)]
-        approx = [mul(left_form(x), y) for x, y in zip(approx, rest)]
+        rest.append(eye - one * start)
+        approx.append((eye + rest[-1]) * start)
+    right = None
+    for step in range(ITERS - 1):
+        if step < 2:
+            rest = [square(e) for e in rest]
+        else:
+            rest = [times(left_form(e), f) for e, f in zip(rest, right)]
+        right = [right_form(e) for e in rest]
+        approx = [x + times(left_form(x), f) for x, f in zip(approx, right)]
     return approx
 
 
 def both_sides(left, w, right):
-    a12, a13 = left_form(left)
-    a1 = a12[:, :N]
-    w1, w2, w3 = thirds(w)
-    main = jnp.dot(a12, jnp.concatenate([w1, w1], axis=0), preferred_element_type=jnp.float32)
-    cross = jnp.dot(a12, jnp.concatenate([w2, w2], axis=0), preferred_element_type=jnp.float32)
-    small = jnp.dot(
-        jnp.concatenate([a1, a13[:, N:]], axis=1),
-        jnp.concatenate([w3, w1], axis=0),
-        preferred_element_type=jnp.float32,
-    )
-    product = main + (cross + small)
-    return jnp.concatenate([mul(left_form(product[:, j * N : (j + 1) * N]), right[j]) for j in range(2)], axis=1)
+    left = left_form(left)
+    parts = []
+    for j in range(2):
+        product = mul(left, w[:, j * N : (j + 1) * N])
+        parts.append(times(left_form(product), right[j]))
+    return jnp.concatenate(parts, axis=1)
 
 
 def group_rows(index, odd_row):
@@ -300,8 +320,13 @@
     return pl.ds(pl.multiple_of(place * N, N), N)
 
 
-def near_kernel(meta, own, damping, weight, rows_out, right_out):
-    core, row, col = meta[0], meta[1], meta[2]
+def number(meta, i):
+    return meta[i].astype(jnp.int32)
+
+
+def near_kernel(meta, own, weight, rows_out, right_out):
+    core, row, col = [number(meta, i) for i in range(3)]
+    damping = meta[7]
     group, odd_row = row // 2, row % 2
 
     def fetch(k):
@@ -311,17 +336,27 @@
     lane = 32 * core + group + 4 * odd_row
     blocks = [unpacked(first, second, diags, lane) for second in range(2)]
     blocks += [unpacked(last, second, diags, 32 * core + 10 + col // 2) for second in range(2)]
-    approx = inverses(blocks, damping[0])
+    approx = inverses(blocks, damping)
+    right = [right_form(one) for one in approx[2:]]
     for i in range(2):
-        rows_out[pl.ds(i * N, N), :] = both_sides(approx[i], weight[group_rows(2 * core + i, odd_row), :], approx[2:])
-        right_out[i] = approx[2 + i]
-
-
-def far_kernel(meta, own, other, damping, weight, rows_in, right_in, out, updated):
-    core, row = meta[0], meta[1]
-    block, slot_half, slot_place, slot_second = meta[3], meta[4], meta[5], meta[6]
+        rows_out[pl.ds(i * N, N), :] = both_sides(approx[i], weight[group_rows(2 * core + i, odd_row), :], right)
+        right_out[i] = right[i]
+
+
+def far_kernel(meta, own, other, weight, rows_in, right_in, out_hbm, updated_hbm, out, updated, sems):
+    core, row = number(meta, 0), number(meta, 1)
+    block, slot_half, slot_place, slot_second = [number(meta, i) for i in range(3, 7)]
+    damping = meta[7]
     group, odd_row = row // 2, row % 2
     fifth_half = group % 2
+    sent = []
+
+    def send(src, dst):
+        sent.append(pltpu.make_async_copy(src, dst, sems.at[len(sent)]))
+        sent[-1].start()
+
+    for i in range(2):
+        send(rows_in.at[pl.ds(i * N, N), :], out_hbm.at[group_rows(2 * core + i, odd_row), :])
 
     def fetch(ref, k):
         return ref[pl.ds(k, N, stride=ROWS), :]
@@ -335,45 +370,52 @@
     mine = jnp.where(slot_half == core, fetch(own, 4 + core), fetch(other, 4 + core))
     fresh = unpacked(mine, slot_second, diags, 32 * slot_half + slot_place)
     updated[0] = jnp.where(block > 0, fresh, 0.0)
-
-    approx = inverses(blocks, damping[0])
+    send(updated, updated_hbm)
+
+    approx = inverses(blocks, damping)
     right = [right_in[0], right_in[1]]
-    for i in range(2):
-        out[group_rows(2 * core + i, odd_row), :] = rows_in[pl.ds(i * N, N), :]
-        at = group_rows(2 * (1 - core) + i, odd_row)
-        out[at, :] = both_sides(approx[i], weight[at, :], right)
-    at = group_rows("fifth", odd_row)
-    out[at, :] = both_sides(approx[2], weight[at, :], right)
-
-
-def apply_near(meta, own, damping, weight):
+    for i in range(3):
+        at = group_rows("fifth" if i == 2 else 2 * (1 - core) + i, odd_row)
+        out[pl.ds(i * N, N), :] = both_sides(approx[i], weight[at, :], right)
+        send(out.at[pl.ds(i * N, N), :], out_hbm.at[at, :])
+    for copy in sent:
+        copy.wait()
+
+
+def apply_near(meta, own, weight):
     vmem, smem = pl.BlockSpec(memory_space=pltpu.VMEM), pl.BlockSpec(memory_space=pltpu.SMEM)
     return pl.pallas_call(
         near_kernel,
         out_shape=(
             jax.ShapeDtypeStruct((2 * N, 2 * N), jnp.float32),
-            jax.ShapeDtypeStruct((2, N, N), jnp.float32),
+            jax.ShapeDtypeStruct((2, 2 * N, 2 * N), jnp.bfloat16),
         ),
-        in_specs=[smem, vmem, smem, vmem],
+        in_specs=[smem, vmem, vmem],
         out_specs=(vmem, vmem),
         compiler_params=pltpu.CompilerParams(vmem_limit_bytes=40 * 2**20),
         name="apply_near",
-    )(meta, own, damping, weight)
-
-
-def apply_far(meta, own, other, damping, weight, rows, right):
+    )(meta, own, weight)
+
+
+def apply_far(meta, own, other, weight, rows, right):
     vmem, smem = pl.BlockSpec(memory_space=pltpu.VMEM), pl.BlockSpec(memory_space=pltpu.SMEM)
+    hbm = pl.BlockSpec(memory_space=pltpu.HBM)
     return pl.pallas_call(
         far_kernel,
         out_shape=(
             jax.ShapeDtypeStruct(weight.shape, jnp.float32),
             jax.ShapeDtypeStruct((1, N, N), jnp.float32),
         ),
-        in_specs=[smem, vmem, vmem, smem, vmem, vmem, vmem],
-        out_specs=(vmem, vmem),
+        in_specs=[smem] + [vmem] * 5,
+        out_specs=(hbm, hbm),
+        scratch_shapes=[
+            pltpu.VMEM((3 * N, 2 * N), jnp.float32),
+            pltpu.VMEM((1, N, N), jnp.float32),
+            pltpu.SemaphoreType.DMA((6,)),
+        ],
         compiler_params=pltpu.CompilerParams(vmem_limit_bytes=40 * 2**20),
         name="apply_far",
-    )(meta, own, other, damping, weight, rows, right)
+    )(meta, own, other, weight, rows, right)
 
 
 def picked_rows(owner, half):
@@ -411,19 +453,18 @@
     slot_half, slot_place = pair_home(jnp.maximum(block - 1, 0))
     slot_second = jnp.maximum(block - 1, 0) % 2
     slot = [block, slot_half, slot_place, slot_second]
-    apply_meta = jnp.stack([core, row, col] + slot).astype(jnp.int32)
+    apply_meta = jnp.stack([one.astype(jnp.float32) for one in [core, row, col] + slot + [damping]])
     picks = picked_rows(owner, core)
 
     got = lax.all_to_all(chip.reshape(16, 8 * TILES, N), PLANE, 0, 0, tiled=True)
     by_depth = plane_sum(got)
     got = lax.all_to_all(by_depth, DEPTH, 0, 0, tiled=True)
-    damping = damping.reshape(1)
-    got, apply_meta, damping = lax.optimization_barrier((got, apply_meta, damping))
+    got, apply_meta = lax.optimization_barrier((got, apply_meta))
     sent = spread_rows(got, picks)
     near = lax.all_to_all(sent.reshape(N, ROWS, 1, N), CHIPS, 0, 0, tiled=True).reshape(ROWS * N, N)
     far = lax.ppermute(near, "c", swap)
-    rows, right = apply_near(apply_meta, near, damping, weight_grad)
-    return apply_far(apply_meta, near, far, damping, weight_grad, rows, right)
+    rows, right = apply_near(apply_meta, near, weight_grad)
+    return apply_far(apply_meta, near, far, weight_grad, rows, right)
 
 
 def solution(mesh):

time: 93.7 us -> 91.1 us (0.972)
  Pallas kernels: 17.4 us -> 15.5 us
    all_to_all x1, waiting for transfers between devices: 22.9 us -> 21.7 us  [on_device(): lax.all_to_all(chip.reshape(16, 8 * TILES, N), PLANE, 0, 0, tiled=True)]
    pallas_call x1, Pallas kernels: 4.5 us -> 3.32 us  [apply_far(): pl.pallas_call(far_kernel, out_shape=(jax.ShapeDtypeStruct(weight.shape,...]
  transfers between devices with their start and end apart: 4 -> 4, of which waited for: 3 -> 3; matrix products, arithmetic and copies ran while one was open for 2% -> 1% of each run, Pallas kernels for 7% -> 6%
where the time goes in v4:
time: 91.1 us; the launch traced here: 90.8 us
  waiting for transfers between devices  29.8 us (33%)
  starting transfers between devices  21.5 us (24%)
  blocking collectives  19.7 us (22%)
  Pallas kernels  15.5 us (17%)
  between operations  2.92 us (3%)
  other arithmetic  0.95 us (1%)
    all_to_all x1, waiting for transfers between devices, on_device(): lax.all_to_all(chip.reshape(16, 8 * TILES, N), PLANE, 0, 0, tiled=True)  21.7 us
    all_to_all x1, blocking collectives, on_device(): lax.all_to_all(sent.reshape(N, ROWS, 1, N), CHIPS, 0, 0, tiled=True)  19.7 us
    all_to_all x1, starting transfers between devices, on_device(): got = lax.all_to_all(by_depth, DEPTH, 0, 0, tiled=True)  8.19 us
    all_to_all x1, waiting for transfers between devices, on_device(): got = lax.all_to_all(by_depth, DEPTH, 0, 0, tiled=True)  7.67 us
    pallas_call x2, Pallas kernels, partials(): pl.pallas_call(functools.partial(partial_kernel, core_of, me_of, own), ou...  7.35 us
    all_to_all x1, starting transfers between devices, on_device(): lax.all_to_all(chip.reshape(16, 8 * TILES, N), PLANE, 0, 0, tiled=True)  5.17 us
    ppermute x1, starting transfers between devices, on_device(): far = lax.ppermute(near, 'c', swap)  4.88 us
    pallas_call x1, Pallas kernels, apply_far(): pl.pallas_call(far_kernel, out_shape=(jax.ShapeDtypeStruct(weight.shape,...  3.32 us
  transfers between devices with their start and end apart: 4, of which 3 were waited for; matrix products, arithmetic and copies ran while one was open for 1% of the time, Pallas kernels for 6%

profile of v4, /device:TPU:1, one launch (start us, length us, event | category | flops | bytes accessed | tf_op | source)
XLA Modules:
  0.0 90.8 jit_solution(8498600000034244217)
XLA Ops:
  0.6 0.0 copy-start.1
  0.6 0.0 copy-start.2
  0.6 4.2 %other_half.1 = f32[16,27,8,128]{3,2,1,0:T(8,128)} custom-call(bf16[256,5120]{1,0:T(8,128)(2,1)} %refs_0_.3, bf16[256,8192]{1,0:T(8,128)(2,1)} %refs_1_.3, f32[1,128,128]{2,1,0:T(8,128)} %refs_2_.3, s32[256]{0:T(256)} %refs_3_.3), custom_call_target="tpu_custom_call" | custom-call | tf_op jit(solution)/shard_map/other_half/pallas_call | solution.py:151
  4.9 3.3 %collective-permute-start = (f32[16,27,8,128]{3,2,1,0:T(8,128)}, f32[16,27,8,128]{3,2,1,0:T(8,128)S(1)}, u32[]{:S(2)}, u32[]{:S(2)}) collective-permute-start(f32[16,27,8,128]{3,2,1,0:T(8,128)} %other_half.1), channel_id=1, source_target_pairs={{0,1},{1,0},{2,3},{3,2},{4,5},{5,4},{6,7},{7,6},{8,9},{9,8},{10,11... | collective-permute-start | bytes 5308424 | tf_op jit(solution)/shard_map/ppermute | solution.py:445
  8.2 0.0 copy-done.1
  8.2 0.0 copy-done.2
  8.2 3.1 %own_half.1.own = f32[16,27,8,128]{3,2,1,0:T(8,128)S(1)} custom-call(bf16[256,5120]{1,0:T(8,128)(2,1)} %refs_0_.3, bf16[256,8192]{1,0:T(8,128)(2,1)} %refs_1_.3, f32[1,128,128]{2,1,0:T(8,128)S(1)} %copy-done.1, s32[256]{0:T(256)S(1)} %copy-done.2), custom_call_target="tpu_custom_call" | custom-call | tf_op jit(solution)/shard_map/own_half/pallas_call | solution.py:151
  11.3 0.4 collective-permute-done.received
  11.7 1.3 %add_cores.1 = f32[16,27,8,128]{3,2,1,0:T(8,128)} custom-call(f32[16,27,8,128]{3,2,1,0:T(8,128)S(1)} %own_half.1.own, f32[16,27,8,128]{3,2,1,0:T(8,128)S(1)} %collective-permute-done.received), custom_call_target="tpu_custom_call" | custom-call | tf_op jit(solution)/shard_map/add_cores/pallas_call | solution.py:178
  13.0 0.0 copy-start.6
  13.0 0.0 copy-start.7
  13.0 0.0 copy-start.3
  13.1 0.0 copy-start.4
  13.1 0.0 copy-start.5
  13.1 5.2 %all-to-all-start = ((f32[16,216,128]{2,1,0:T(8,128)}), f32[16,216,128]{2,1,0:T(8,128)S(1)}, u32[]{:S(2)}, u32[]{:S(2)}) async-start(f32[16,216,128]{2,1,0:T(8,128)} %bitcast), calls=%async_computation | async-start | bytes 3538944 | tf_op jit(solution)/shard_map/all_to_all | solution.py:459
  18.3 0.6 fusion.5
  21.0 0.0 copy-done.6
  21.0 0.0 copy-done.7
  21.0 0.1 select_reduce_fusion
  21.2 0.0 copy-done.3
  21.2 0.0 copy-done.4
  21.2 0.0 copy-done.5
  21.2 0.1 copy.17
  21.3 0.1 eq.97
  21.5 0.0 copy-start
  21.5 21.7 %all-to-all-done.got = f32[16,216,128]{2,1,0:T(8,128)S(1)} async-done(((f32[16,216,128]{2,1,0:T(8,128)}), f32[16,216,128]{2,1,0:T(8,128)S(1)}, u32[]{:S(2)}, u32[]{:S(2)}) %all-to-all-start) | async-done | bytes 1769504 | tf_op jit(solution)/shard_map/all_to_all | solution.py:459
  43.2 0.8 plane_sum.1
  44.0 8.2 %all-to-all-start.1 = ((f32[8,32,128]{2,1,0:T(8,128)}), f32[8,32,128]{2,1,0:T(8,128)S(1)}, u32[]{:S(2)}, u32[]{:S(2)}) async-start(f32[8,32,128]{2,1,0:T(8,128)} %plane_sum.1), calls=%async_computation.1 | async-start | bytes 262144 | tf_op jit(solution)/shard_map/all_to_all | solution.py:461
  52.1 0.1 stack.56.meta
  52.2 0.2 compare_convert_fusion.picks
  52.4 7.7 %all-to-all-done.1.got = f32[8,32,128]{2,1,0:T(8,128)S(1)} async-done(((f32[8,32,128]{2,1,0:T(8,128)}), f32[8,32,128]{2,1,0:T(8,128)S(1)}, u32[]{:S(2)}, u32[]{:S(2)}) %all-to-all-start.1) | async-done | bytes 131104 | tf_op jit(solution)/shard_map/all_to_all | solution.py:461
  60.1 0.2 spread_rows.1
  60.3 19.7 %all_to_all.15 = f32[128,6,1,128]{3,2,1,0:T(1,128)S(1)} all-to-all(f32[128,6,1,128]{3,2,1,0:T(1,128)S(1)} %bitcast.17), channel_id=1, replica_groups=mesh['zh'=2,'x'=4,'zl'=4,'y'=4,'c'=2] {'x','y','zh','zl'}, dimensions={0} | all-to-all | bytes 786432 | tf_op jit(solution)/shard_map/all_to_all | solution.py:464
  80.0 4.9 %collective-permute-start.1 = (f32[768,128]{1,0:T(8,128)S(1)}, f32[768,128]{1,0:T(8,128)S(1)}, u32[]{:S(2)}, u32[]{:S(2)}) collective-permute-start(f32[768,128]{1,0:T(8,128)S(1)} %bitcast.14), channel_id=1, source_target_pairs={{0,1},{1,0},{2,3},{3,2},{4,5},{5,4},{6,7},{7,6},{8,9},{9,8},{10,11... | collective-permute-start | bytes 1179656 | tf_op jit(solution)/shard_map/ppermute | solution.py:465
  84.8 0.0 copy-done
  84.8 2.6 %apply_near.1 = (f32[256,256]{1,0:T(8,128)S(1)}, bf16[2,256,256]{2,1,0:T(8,128)(2,1)S(1)}) custom-call(f32[8]{0:T(128)S(1)} %stack.56.meta, f32[768,128]{1,0:T(8,128)S(1)} %bitcast.15, f32[640,256]{1,0:T(8,128)S(1)} %copy-done), custom_call_target="tpu_custom_call" | custom-call | tf_op jit(solution)/shard_map/apply_near/pallas_call | solution.py:387
  87.4 0.0 collective-permute-done.1.other
  87.4 3.3 %apply_far.1 = (f32[640,256]{1,0:T(8,128)}, f32[1,128,128]{2,1,0:T(8,128)}) custom-call(f32[8]{0:T(128)S(1)} %stack.56.meta, f32[768,128]{1,0:T(8,128)S(1)} %bitcast.16, f32[768,128]{1,0:T(8,128)S(1)} %collective-permute-done.1.other, f32[640,256]{1,0:T(8,128)S(1)} %copy-done, f32[256,256]{1,0:T(8,128)S(1)} %get-tuple-element.10.rows_in, ...), custom_call_target="tpu_custom_call" | custom-call | tf_op jit(solution)/shard_map/apply_far/pallas_call | solution.py:403
  (4 shorter events, 0.1 us)
Async XLA Ops:
  0.6 7.5 %copy-start.1 = (f32[1,128,128]{2,1,0:T(8,128)S(1)}, f32[1,128,128]{2,1,0:T(8,128)}, u32[]{:S(2)}) copy-start(f32[1,128,128]{2,1,0:T(8,128)} %refs_2_.3) | copy-start | bytes 196612
  0.6 7.5 %copy-start.2 = (s32[256]{0:T(256)S(1)}, s32[256]{0:T(256)}, u32[]{:S(2)}) copy-start(s32[256]{0:T(256)} %refs_3_.3) | copy-start | bytes 3076
  4.9 6.8 %collective-permute-start = (f32[16,27,8,128]{3,2,1,0:T(8,128)}, f32[16,27,8,128]{3,2,1,0:T(8,128)S(1)}, u32[]{:S(2)}, u32[]{:S(2)}) collective-permute-start(f32[16,27,8,128]{3,2,1,0:T(8,128)} %other_half.1), channel_id=1, source_target_pairs={{0,1},{1,0},{2,3},{3,2},{4,5},{5,4},{6,7},{7,6},{8,9},{9,8},{10,11... | collective-permute-start | bytes 5308424 | tf_op jit(solution)/shard_map/ppermute | solution.py:445
  13.0 8.0 %copy-start.6 = (s32[128]{0:T(128)S(1)}, s32[128]{0:T(128)}, u32[]{:S(2)}) copy-start(s32[128]{0:T(128)} %constant.183.clone) | copy-start | bytes 1540
  13.0 8.0 %copy-start.7 = (s32[128]{0:T(128)S(1)}, s32[128]{0:T(128)}, u32[]{:S(2)}) copy-start(s32[128]{0:T(128)} %constant.184.clone) | copy-start | bytes 1540
  13.0 8.1 %copy-start.3 = (s32[128,1]{0,1:T(1,128)S(1)}, s32[128,1]{0,1:T(1,128)}, u32[]{:S(2)}) copy-start(s32[128,1]{0,1:T(1,128)} %constant.190) | copy-start | bytes 1540
  13.1 8.1 %copy-start.4 = (s32[128,1]{0,1:T(1,128)S(1)}, s32[128,1]{0,1:T(1,128)}, u32[]{:S(2)}) copy-start(s32[128,1]{0,1:T(1,128)} %constant.191) | copy-start | bytes 1540
  13.1 8.1 %copy-start.5 = (s32[128,1]{0,1:T(1,128)S(1)}, s32[128,1]{0,1:T(1,128)}, u32[]{:S(2)}) copy-start(s32[128,1]{0,1:T(1,128)} %constant.192) | copy-start | bytes 1540
  13.1 30.1 %all-to-all-start = ((f32[16,216,128]{2,1,0:T(8,128)}), f32[16,216,128]{2,1,0:T(8,128)S(1)}, u32[]{:S(2)}, u32[]{:S(2)}) async-start(f32[16,216,128]{2,1,0:T(8,128)} %bitcast), calls=%async_computation | async-start | bytes 3538944 | tf_op jit(solution)/shard_map/all_to_all | solution.py:459
  21.5 63.4 %copy-start = (f32[640,256]{1,0:T(8,128)S(1)}, f32[640,256]{1,0:T(8,128)}, u32[]{:S(2)}) copy-start(f32[640,256]{1,0:T(8,128)} %weight.3) | copy-start | bytes 1966084
  44.0 16.1 %all-to-all-start.1 = ((f32[8,32,128]{2,1,0:T(8,128)}), f32[8,32,128]{2,1,0:T(8,128)S(1)}, u32[]{:S(2)}, u32[]{:S(2)}) async-start(f32[8,32,128]{2,1,0:T(8,128)} %plane_sum.1), calls=%async_computation.1 | async-start | bytes 262144 | tf_op jit(solution)/shard_map/all_to_all | solution.py:461
  80.0 7.5 %collective-permute-start.1 = (f32[768,128]{1,0:T(8,128)S(1)}, f32[768,128]{1,0:T(8,128)S(1)}, u32[]{:S(2)}, u32[]{:S(2)}) collective-permute-start(f32[768,128]{1,0:T(8,128)S(1)} %bitcast.14), channel_id=1, source_target_pairs={{0,1},{1,0},{2,3},{3,2},{4,5},{5,4},{6,7},{7,6},{8,9},{9,8},{10,11... | collective-permute-start | bytes 1179656 | tf_op jit(solution)/shard_map/ppermute | solution.py:465

commit v5 on v4

--- a/solution.py
+++ b/solution.py
@@ -62,11 +62,38 @@
 
 
 GROUPS = (12, 14)
+META = 5
+
+
+def wanted_slots():
+    at = lax.broadcasted_iota(jnp.int32, (ROWS * N, N), 0)
+    chip = (at * 10923) >> 16
+    kind = at - ROWS * chip
+    x, y, z_hi, z_lo = chip >> 5, (chip >> 3) & 3, (chip >> 2) & 1, chip & 3
+    slot = (z_hi * 4 + x) * 32 + (z_lo * 4 + y) * 2 + kind - 4
+    return jnp.where(kind < 4, -1, slot)
+
+
+def fixed_picks():
+    x, y, zh, zl = np.unravel_index(np.arange(N), (4, 4, 2, 4))
+    row, pair_col = zh * 4 + x, zl * 4 + y
+    none = np.full(N, 99)
+    places = [row // 2 + 4 * (row % 2), 8 + row // 4, 10 + pair_col, np.full(N, HALF), none, none]
+    wanted = np.arange(96) % 32
+    base = np.stack(places, axis=1).reshape(ROWS * N, 1) == wanted
+    homes = np.zeros((2, N, 96), bool)
+    for half in range(2):
+        for place in range(HALF):
+            which, pair = pair_column(place, half)
+            first = (NA if which else 0) + 2 * pair
+            homes[half, first : first + 2] = wanted == place
+    return jnp.asarray(base, jnp.bfloat16), jnp.asarray(homes, jnp.bfloat16)
 
 
 def partial_kernel(core_of, me_of, own, *refs):
     if own:
-        acts, outgrads, prev_hbm, owner_hbm, out, buf, prev, owner, rows, sems, small_sems = refs
+        acts, outgrads, prev_hbm, owner_hbm, owner_row, damping, base, homes = refs[:8]
+        out, picks, meta, buf, prev, owner, rows, sems, small_sems = refs[8:]
     else:
         acts, outgrads, prev_hbm, owner_hbm, out_hbm, buf, prev, owner, rows, sems, small_sems, out, out_sems = refs
     core, me = core_of(), me_of()
@@ -95,6 +122,14 @@
     slot_half, slot_place = pair_home(slot)
     second_of = slot % 2
 
+    if own:
+        for i, one in enumerate([block, slot_half, slot_place, second_of]):
+            meta[i] = jnp.int32(one).astype(jnp.float32)
+        meta[META - 1] = damping[0]
+        matches = (wanted_slots() == owner_row[0:1, :]).astype(jnp.float32).astype(jnp.bfloat16)
+        found = jnp.dot(matches, homes[core], preferred_element_type=jnp.float32)
+        picks[...] = (base[...].astype(jnp.float32) + found).astype(jnp.bfloat16)
+
     done, sent = 0, []
     for number, count in enumerate(GROUPS):
         begin, end = done, done + count
@@ -133,8 +168,13 @@
         copy.wait()
 
 
-def partials(acts, outgrads, prev, owner, core_of, me_of, own):
+def partials(acts, outgrads, prev, owner, core_of, me_of, damping=None):
+    own = damping is not None
     hbm, vmem = pl.BlockSpec(memory_space=pltpu.HBM), pl.BlockSpec(memory_space=pltpu.VMEM)
+    smem = pl.BlockSpec(memory_space=pltpu.SMEM)
+    shape = jax.ShapeDtypeStruct((16, TILES, 8, N), jnp.float32)
+    picks_shape = jax.ShapeDtypeStruct((ROWS * N, 96), jnp.bfloat16)
+    meta_shape = jax.ShapeDtypeStruct((META,), jnp.float32)
     scratch = [
         pltpu.VMEM((HALF, 256, 2 * N), jnp.bfloat16),
         pltpu.VMEM((1, N, N), jnp.float32),
@@ -150,37 +190,26 @@
         ]
     return pl.pallas_call(
         functools.partial(partial_kernel, core_of, me_of, own),
-        out_shape=jax.ShapeDtypeStruct((16, TILES, 8, N), jnp.float32),
-        in_specs=[hbm] * 4,
-        out_specs=vmem if own else hbm,
+        out_shape=(shape, picks_shape, meta_shape) if own else shape,
+        in_specs=[hbm] * 4 + ([vmem, smem, vmem, vmem] if own else []),
+        out_specs=(vmem, vmem, smem) if own else hbm,
         scratch_shapes=scratch,
         compiler_params=pltpu.CompilerParams(vmem_limit_bytes=(50 if own else 61) * 2**20),
         name="own_half" if own else "other_half",
-    )(acts, outgrads, prev, owner)
-
-
-CHUNKS = 4
-
-
-def add_kernel(own, received, out_hbm, out, sems):
-    copies = []
-    for i in range(CHUNKS):
-        at = pl.ds(i * (16 // CHUNKS), 16 // CHUNKS)
-        out[at] = own[at] + received[at]
-        copies.append(pltpu.make_async_copy(out.at[at], out_hbm.at[at], sems.at[i]))
-        copies[-1].start()
-    for copy in copies:
-        copy.wait()
+    )(*((acts, outgrads, prev, owner) + ((owner.reshape(2, N), damping) + fixed_picks() if own else ())))
+
+
+def add_kernel(a, b, out):
+    out[...] = a[...] + b[...]
 
 
 def add_cores(own, received):
-    hbm, vmem = pl.BlockSpec(memory_space=pltpu.HBM), pl.BlockSpec(memory_space=pltpu.VMEM)
+    vmem = pl.BlockSpec(memory_space=pltpu.VMEM)
     return pl.pallas_call(
         add_kernel,
         out_shape=jax.ShapeDtypeStruct(own.shape, jnp.float32),
         in_specs=[vmem, vmem],
-        out_specs=hbm,
-        scratch_shapes=[pltpu.VMEM(own.shape, jnp.float32), pltpu.SemaphoreType.DMA((CHUNKS,))],
+        out_specs=vmem,
         compiler_params=pltpu.CompilerParams(vmem_limit_bytes=16 * 2**20),
         name="add_cores",
     )(own, received)
@@ -259,17 +288,17 @@
     return times(left, right_form(b))
 
 
-def square(e):
+def correction(e):
     e1 = e.astype(jnp.bfloat16)
     low = e - e1.astype(jnp.float32)
-    e2 = low.astype(jnp.bfloat16)
-    e3 = (low - e2.astype(jnp.float32)).astype(jnp.bfloat16)
-    wide = jnp.concatenate([jnp.concatenate([e1, e2], axis=1), jnp.concatenate([e2, e1], axis=1)], axis=0)
-    four = jnp.dot(jnp.concatenate([e1, e2], axis=1), wide, preferred_element_type=jnp.float32)
-    two = jnp.dot(
+    e3 = (low - low.astype(jnp.bfloat16).astype(jnp.float32)).astype(jnp.bfloat16)
+    return jnp.dot(
         jnp.concatenate([e1, e3], axis=1), jnp.concatenate([e3, e1], axis=0), preferred_element_type=jnp.float32
     )
-    return four[:, :N] + (four[:, N:] + two)
+
+
+def square(e):
+    return mul(left_form(e), e) + correction(e)
 
 
 def unpacked(packed, second, diags, lane):
@@ -295,15 +324,20 @@
         start = 1.0 / bound
         rest.append(eye - one * start)
         approx.append((eye + rest[-1]) * start)
-    right = None
-    for step in range(ITERS - 1):
-        if step < 2:
-            rest = [square(e) for e in rest]
+    rest = [square(e) for e in rest]
+    for step in range(1, ITERS):
+        right = [right_form(e) for e in rest]
+        if step == ITERS - 1:
+            return [x + times(left_form(x), f) for x, f in zip(approx, right)]
+        stacked = [
+            times(jnp.concatenate([left_form(e), left_form(x)], axis=0), f)
+            for e, x, f in zip(rest, approx, right)
+        ]
+        approx = [x + both[N:] for x, both in zip(approx, stacked)]
+        if step == 1:
+            rest = [both[:N] + correction(e) for e, both in zip(rest, stacked)]
         else:
-            rest = [times(left_form(e), f) for e, f in zip(rest, right)]
-        right = [right_form(e) for e in rest]
-        approx = [x + times(left_form(x), f) for x, f in zip(approx, right)]
-    return approx
+            rest = [both[:N] for both in stacked]
 
 
 def both_sides(left, w, right):
@@ -324,9 +358,10 @@
     return meta[i].astype(jnp.int32)
 
 
-def near_kernel(meta, own, weight, rows_out, right_out):
-    core, row, col = [number(meta, i) for i in range(3)]
-    damping = meta[7]
+def near_kernel(places, meta_hbm, own, weight, rows_out, right_out, meta, meta_sem):
+    scalars = pltpu.make_async_copy(meta_hbm, meta, meta_sem.at[0])
+    scalars.start()
+    core, row, col = [place() for place in places]
     group, odd_row = row // 2, row % 2
 
     def fetch(k):
@@ -336,17 +371,19 @@
     lane = 32 * core + group + 4 * odd_row
     blocks = [unpacked(first, second, diags, lane) for second in range(2)]
     blocks += [unpacked(last, second, diags, 32 * core + 10 + col // 2) for second in range(2)]
-    approx = inverses(blocks, damping)
+    scalars.wait()
+    approx = inverses(blocks, meta[4])
     right = [right_form(one) for one in approx[2:]]
     for i in range(2):
         rows_out[pl.ds(i * N, N), :] = both_sides(approx[i], weight[group_rows(2 * core + i, odd_row), :], right)
         right_out[i] = right[i]
 
 
-def far_kernel(meta, own, other, weight, rows_in, right_in, out_hbm, updated_hbm, out, updated, sems):
-    core, row = number(meta, 0), number(meta, 1)
-    block, slot_half, slot_place, slot_second = [number(meta, i) for i in range(3, 7)]
-    damping = meta[7]
+def far_kernel(places, meta_hbm, own, other, weight, rows_in, right_in, out_hbm, updated_hbm, *scratch):
+    out, updated, meta, meta_sem, sems = scratch
+    scalars = pltpu.make_async_copy(meta_hbm, meta, meta_sem.at[0])
+    scalars.start()
+    core, row, _ = [place() for place in places]
     group, odd_row = row // 2, row % 2
     fifth_half = group % 2
     sent = []
@@ -367,12 +404,14 @@
     lane = 32 * (1 - core) + group + 4 * odd_row
     blocks = [unpacked(first, second, diags, lane) for second in range(2)]
     blocks.append(unpacked(fifth, odd_row, diags, 32 * fifth_half + 8 + group // 2))
+    scalars.wait()
+    block, slot_half, slot_place, slot_second = [number(meta, i) for i in range(4)]
     mine = jnp.where(slot_half == core, fetch(own, 4 + core), fetch(other, 4 + core))
     fresh = unpacked(mine, slot_second, diags, 32 * slot_half + slot_place)
     updated[0] = jnp.where(block > 0, fresh, 0.0)
     send(updated, updated_hbm)
 
-    approx = inverses(blocks, damping)
+    approx = inverses(blocks, meta[4])
     right = [right_in[0], right_in[1]]
     for i in range(3):
         at = group_rows("fifth" if i == 2 else 2 * (1 - core) + i, odd_row)
@@ -382,35 +421,37 @@
         copy.wait()
 
 
-def apply_near(meta, own, weight):
-    vmem, smem = pl.BlockSpec(memory_space=pltpu.VMEM), pl.BlockSpec(memory_space=pltpu.SMEM)
-    return pl.pallas_call(
-        near_kernel,
+def apply_near(places, meta, own, weight):
+    vmem, hbm = pl.BlockSpec(memory_space=pltpu.VMEM), pl.BlockSpec(memory_space=pltpu.HBM)
+    return pl.pallas_call(
+        functools.partial(near_kernel, places),
         out_shape=(
             jax.ShapeDtypeStruct((2 * N, 2 * N), jnp.float32),
             jax.ShapeDtypeStruct((2, 2 * N, 2 * N), jnp.bfloat16),
         ),
-        in_specs=[smem, vmem, vmem],
+        in_specs=[hbm, vmem, vmem],
         out_specs=(vmem, vmem),
+        scratch_shapes=[pltpu.SMEM((META,), jnp.float32), pltpu.SemaphoreType.DMA((1,))],
         compiler_params=pltpu.CompilerParams(vmem_limit_bytes=40 * 2**20),
         name="apply_near",
     )(meta, own, weight)
 
 
-def apply_far(meta, own, other, weight, rows, right):
-    vmem, smem = pl.BlockSpec(memory_space=pltpu.VMEM), pl.BlockSpec(memory_space=pltpu.SMEM)
-    hbm = pl.BlockSpec(memory_space=pltpu.HBM)
-    return pl.pallas_call(
-        far_kernel,
+def apply_far(places, meta, own, other, weight, rows, right):
+    vmem, hbm = pl.BlockSpec(memory_space=pltpu.VMEM), pl.BlockSpec(memory_space=pltpu.HBM)
+    return pl.pallas_call(
+        functools.partial(far_kernel, places),
         out_shape=(
             jax.ShapeDtypeStruct(weight.shape, jnp.float32),
             jax.ShapeDtypeStruct((1, N, N), jnp.float32),
         ),
-        in_specs=[smem] + [vmem] * 5,
+        in_specs=[hbm] + [vmem] * 5,
         out_specs=(hbm, hbm),
         scratch_shapes=[
             pltpu.VMEM((3 * N, 2 * N), jnp.float32),
             pltpu.VMEM((1, N, N), jnp.float32),
+            pltpu.SMEM((META,), jnp.float32),
+            pltpu.SemaphoreType.DMA((1,)),
             pltpu.SemaphoreType.DMA((6,)),
         ],
         compiler_params=pltpu.CompilerParams(vmem_limit_bytes=40 * 2**20),
@@ -418,53 +459,27 @@
     )(meta, own, other, weight, rows, right)
 
 
-def picked_rows(owner, half):
-    x, y, zh, zl = np.unravel_index(np.arange(N), (4, 4, 2, 4))
-    row, pair_col = zh * 4 + x, zl * 4 + y
-    group, odd_row = row // 2, row % 2
-    fixed = [group + 4 * odd_row, 8 + group // 2, 10 + pair_col, np.full(N, HALF)]
-    halves, places = pair_home(jnp.arange(NB, dtype=jnp.int32))
-    slots = []
-    for core in range(2):
-        slot = jnp.asarray(row * 32 + pair_col * 2 + core, jnp.int32)
-        matches = (owner[:NB, None] == slot[None, :]) & (halves == half)[:, None]
-        slots.append(jnp.sum(jnp.where(matches, places[:, None], 0), axis=0))
-    rows = jnp.stack([jnp.asarray(f) for f in fixed] + slots, axis=1).astype(jnp.int32)
-    wanted = jnp.arange(96, dtype=jnp.int32) % 32
-    return (rows[:, :, None] == wanted).astype(jnp.bfloat16).reshape(ROWS * N, 96)
-
-
 def on_device(acts, outgrads, weight_grad, prev_factor, damping, owner):
     core_of = lambda: lax.axis_index("c").astype(jnp.int32)
     row_of = lambda: lax.axis_index(("zh", "x")).astype(jnp.int32)
     col_of = lambda: lax.axis_index(("zl", "y", "c")).astype(jnp.int32)
     me_of = lambda: row_of() * 32 + col_of()
 
+    places = (core_of, row_of, col_of)
     swap = [(0, 1), (1, 0)]
-    other = partials(acts, outgrads, prev_factor, owner, core_of, me_of, False)
+    other = partials(acts, outgrads, prev_factor, owner, core_of, me_of)
     received = lax.ppermute(other, "c", swap)
-    own = partials(acts, outgrads, prev_factor, owner, core_of, me_of, True)
+    own, picks, apply_meta = partials(acts, outgrads, prev_factor, owner, core_of, me_of, damping.reshape(1))
     chip = add_cores(own, received)
-
-    owner, _ = lax.optimization_barrier((owner, other))
-    core, row, col, me = core_of(), row_of(), col_of(), me_of()
-    numbers = jnp.arange(NB, dtype=jnp.int32)
-    block = jnp.sum(jnp.where(owner[:NB] == me, numbers + 1, 0))
-    slot_half, slot_place = pair_home(jnp.maximum(block - 1, 0))
-    slot_second = jnp.maximum(block - 1, 0) % 2
-    slot = [block, slot_half, slot_place, slot_second]
-    apply_meta = jnp.stack([one.astype(jnp.float32) for one in [core, row, col] + slot + [damping]])
-    picks = picked_rows(owner, core)
 
     got = lax.all_to_all(chip.reshape(16, 8 * TILES, N), PLANE, 0, 0, tiled=True)
     by_depth = plane_sum(got)
     got = lax.all_to_all(by_depth, DEPTH, 0, 0, tiled=True)
-    got, apply_meta = lax.optimization_barrier((got, apply_meta))
     sent = spread_rows(got, picks)
     near = lax.all_to_all(sent.reshape(N, ROWS, 1, N), CHIPS, 0, 0, tiled=True).reshape(ROWS * N, N)
     far = lax.ppermute(near, "c", swap)
-    rows, right = apply_near(apply_meta, near, weight_grad)
-    return apply_far(apply_meta, near, far, weight_grad, rows, right)
+    rows, right = apply_near(places, apply_meta, near, weight_grad)
+    return apply_far(places, apply_meta, near, far, weight_grad, rows, right)
 
 
 def solution(mesh):

time: 91.1 us -> 88.5 us (0.971)
  blocking collectives: 19.7 us -> 65.6 us
  waiting for transfers between devices: 29.8 us -> 0.01 us
  starting transfers between devices: 21.5 us -> 7.52 us
  Pallas kernels: 15.5 us -> 13.8 us
  between operations: 2.92 us -> 1.4 us
  other arithmetic: 0.95 us -> 0 us
    all_to_all x0 -> x2, blocking collectives: none -> 45.1 us  [the longest x1 29 us: on_device(): lax.all_to_all(chip.reshape(16, 8 * TILES, N), PLANE, 0, 0, tiled=True)]
    all_to_all x2 -> x0, waiting for transfers between devices: 29.4 us -> none  [the longest x1 21.7 us: on_device(): lax.all_to_all(chip.reshape(16, 8 * TILES, N), PLANE, 0, 0, tiled=True)]
    all_to_all x2 -> x0, starting transfers between devices: 13.4 us -> none  [the longest x1 8.19 us: on_device(): got = lax.all_to_all(by_depth, DEPTH, 0, 0, tiled=True)]
    pallas_call x1, Pallas kernels: 1.31 us -> 0.26 us  [add_cores(): pl.pallas_call(add_kernel, out_shape=jax.ShapeDtypeStruct(own.shape, jnp....]
  transfers between devices with their start and end apart: 4 -> 2, of which waited for: 3 -> 0; matrix products, arithmetic and copies ran while one was open for 1% -> 0% of each run, Pallas kernels for 6% -> 7%
where the time goes in v5:
time: 88.5 us; the launch traced here: 88.3 us
  blocking collectives  65.6 us (74%)
  Pallas kernels  13.8 us (16%)
  starting transfers between devices  7.52 us (8%)
  between operations  1.4 us (2%)
    all_to_all x1, blocking collectives, on_device(): lax.all_to_all(chip.reshape(16, 8 * TILES, N), PLANE, 0, 0, tiled=True)  29 us
    all_to_all x1, blocking collectives, on_device(): lax.all_to_all(sent.reshape(N, ROWS, 1, N), CHIPS, 0, 0, tiled=True)  20.5 us
    all_to_all x1, blocking collectives, on_device(): got = lax.all_to_all(by_depth, DEPTH, 0, 0, tiled=True)  16.1 us
    pallas_call x2, Pallas kernels, partials(): pl.pallas_call(functools.partial(partial_kernel, core_of, me_of, own), ou...  7.94 us
    ppermute x1, starting transfers between devices, on_device(): far = lax.ppermute(near, 'c', swap)  4.2 us
    ppermute x1, starting transfers between devices, on_device(): received = lax.ppermute(other, 'c', swap)  3.32 us
    pallas_call x1, Pallas kernels, apply_far(): pl.pallas_call(functools.partial(far_kernel, places), out_shape=(jax.Shap...  3.03 us
    pallas_call x1, Pallas kernels, apply_near(): pl.pallas_call(functools.partial(near_kernel, places), out_shape=(jax.Sha...  2.27 us
  transfers between devices with their start and end apart: 2, of which 0 were waited for; matrix products, arithmetic and copies ran while one was open for 0% of the time, Pallas kernels for 7%

profile of v5, /device:TPU:1, one launch (start us, length us, event | category | flops | bytes accessed | tf_op | source)
XLA Modules:
  0.0 88.3 jit_solution(17413766346855893779)
XLA Ops:
  0.6 0.0 copy-start.2
  0.6 0.0 copy-start.3
  0.7 0.0 copy-start.4
  0.7 0.0 copy-start.1
  0.7 4.3 %other_half.1 = f32[16,27,8,128]{3,2,1,0:T(8,128)} custom-call(bf16[256,5120]{1,0:T(8,128)(2,1)} %refs_0_.3, bf16[256,8192]{1,0:T(8,128)(2,1)} %refs_1_.3, f32[1,128,128]{2,1,0:T(8,128)} %refs_2_.3, s32[256]{0:T(256)} %refs_3_.3), custom_call_target="tpu_custom_call" | custom-call | tf_op jit(solution)/shard_map/other_half/pallas_call | solution.py:191
  5.0 3.3 %collective-permute-start = (f32[16,27,8,128]{3,2,1,0:T(8,128)}, f32[16,27,8,128]{3,2,1,0:T(8,128)S(1)}, u32[]{:S(2)}, u32[]{:S(2)}) collective-permute-start(f32[16,27,8,128]{3,2,1,0:T(8,128)} %other_half.1), channel_id=1, source_target_pairs={{0,1},{1,0},{2,3},{3,2},{4,5},{5,4},{6,7},{7,6},{8,9},{9,8},{10,11... | collective-permute-start | bytes 5308424 | tf_op jit(solution)/shard_map/ppermute | solution.py:471
  8.9 0.0 copy-done.2
  8.9 0.0 copy-done.3
  8.9 0.0 copy-done.4
  9.0 0.0 copy-done.1
  9.0 3.7 %own_half.1 = (f32[16,27,8,128]{3,2,1,0:T(8,128)S(1)}, bf16[768,96]{1,0:T(8,128)(2,1)S(1)}, f32[5]{0:T(128)S(1)}) custom-call(bf16[256,5120]{1,0:T(8,128)(2,1)} %refs_0_.3, bf16[256,8192]{1,0:T(8,128)(2,1)} %refs_1_.3, f32[1,128,128]{2,1,0:T(8,128)S(1)} %copy-done.1, s32[256]{0:T(256)S(1)} %copy-done.4, s32[2,128]{1,0:T(2,128)S(1)} %bitcast.11, ...), custom_call_target="tpu_custom_call" | custom-call | tf_op jit(solution)/shard_map/own_half/pallas_call | solution.py:191
  12.6 0.0 collective-permute-done.b
  12.7 0.3 add_cores.1
  12.9 29.0 %all_to_all.15.got = f32[16,216,128]{2,1,0:T(8,128)S(1)} all-to-all(f32[16,216,128]{2,1,0:T(8,128)S(1)} %bitcast.6), channel_id=1, replica_groups=mesh['zh'=2,'x'=4,'zl'=4,'y'=4,'c'=2] {'x','y'}, dimensions={0} | all-to-all | bytes 3538944 | tf_op jit(solution)/shard_map/all_to_all | solution.py:475
  41.9 0.0 copy-start
  41.9 0.1 plane_sum.1
  42.0 16.1 %all_to_all.16.got = f32[8,32,128]{2,1,0:T(8,128)S(1)} all-to-all(f32[8,32,128]{2,1,0:T(8,128)S(1)} %plane_sum.1), channel_id=1, replica_groups=mesh['zh'=2,'x'=4,'zl'=4,'y'=4,'c'=2] {'zh','zl'}, dimensions={0} | all-to-all | bytes 262144 | tf_op jit(solution)/shard_map/all_to_all | solution.py:477
  58.1 0.2 spread_rows.1
  58.3 20.5 %all_to_all.17 = f32[128,6,1,128]{3,2,1,0:T(1,128)S(1)} all-to-all(f32[128,6,1,128]{3,2,1,0:T(1,128)S(1)} %bitcast.10), channel_id=1, replica_groups=mesh['zh'=2,'x'=4,'zl'=4,'y'=4,'c'=2] {'x','y','zh','zl'}, dimensions={0} | all-to-all | bytes 786432 | tf_op jit(solution)/shard_map/all_to_all | solution.py:479
  78.8 4.2 %collective-permute-start.1 = (f32[768,128]{1,0:T(8,128)S(1)}, f32[768,128]{1,0:T(8,128)S(1)}, u32[]{:S(2)}, u32[]{:S(2)}) collective-permute-start(f32[768,128]{1,0:T(8,128)S(1)} %bitcast.7), channel_id=1, source_target_pairs={{0,1},{1,0},{2,3},{3,2},{4,5},{5,4},{6,7},{7,6},{8,9},{9,8},{10,11... | collective-permute-start | bytes 1179656 | tf_op jit(solution)/shard_map/ppermute | solution.py:480
  83.0 0.0 copy-done
  83.0 2.3 %apply_near.1 = (f32[256,256]{1,0:T(8,128)S(1)}, bf16[2,256,256]{2,1,0:T(8,128)(2,1)S(1)}) custom-call(f32[5]{0:T(128)S(1)} %get-tuple-element.7.meta_hbm, f32[768,128]{1,0:T(8,128)S(1)} %bitcast.8, f32[640,256]{1,0:T(8,128)S(1)} %copy-done), custom_call_target="tpu_custom_call" | custom-call | tf_op jit(solution)/shard_map/apply_near/pallas_call | solution.py:426
  85.3 0.0 collective-permute-done.1.other
  85.3 3.0 %apply_far.1 = (f32[640,256]{1,0:T(8,128)}, f32[1,128,128]{2,1,0:T(8,128)}) custom-call(f32[5]{0:T(128)S(1)} %get-tuple-element.7.meta_hbm, f32[768,128]{1,0:T(8,128)S(1)} %bitcast.9, f32[768,128]{1,0:T(8,128)S(1)} %collective-permute-done.1.other, f32[640,256]{1,0:T(8,128)S(1)} %copy-done, f32[256,256]{1,0:T(8,128)S(1)} %get-tuple-element.10.rows_in, ...), custom_call_target="tpu_custom_call" | custom-call | tf_op jit(solution)/shard_map/apply_far/pallas_call | solution.py:442
Async XLA Ops:
  0.6 8.3 %copy-start.2 = (bf16[768,96]{1,0:T(8,128)(2,1)S(1)}, bf16[768,96]{1,0:T(8,128)(2,1)}, u32[]{:S(2)}) copy-start(bf16[768,96]{1,0:T(8,128)(2,1)} %constant.4.clone.refs_6_) | copy-start | bytes 442372
  0.6 8.3 %copy-start.3 = (bf16[2,128,96]{2,1,0:T(8,128)(2,1)S(1)}, bf16[2,128,96]{2,1,0:T(8,128)(2,1)}, u32[]{:S(2)}) copy-start(bf16[2,128,96]{2,1,0:T(8,128)(2,1)} %constant.5.clone.refs_7_) | copy-start | bytes 147460
  0.7 8.3 %copy-start.4 = (s32[256]{0:T(256)S(1)}, s32[256]{0:T(256)}, u32[]{:S(2)}) copy-start(s32[256]{0:T(256)} %refs_3_.3) | copy-start | bytes 3076
  0.7 8.3 %copy-start.1 = (f32[1,128,128]{2,1,0:T(8,128)S(1)}, f32[1,128,128]{2,1,0:T(8,128)}, u32[]{:S(2)}) copy-start(f32[1,128,128]{2,1,0:T(8,128)} %refs_2_.3) | copy-start | bytes 196612
  5.0 7.7 %collective-permute-start = (f32[16,27,8,128]{3,2,1,0:T(8,128)}, f32[16,27,8,128]{3,2,1,0:T(8,128)S(1)}, u32[]{:S(2)}, u32[]{:S(2)}) collective-permute-start(f32[16,27,8,128]{3,2,1,0:T(8,128)} %other_half.1), channel_id=1, source_target_pairs={{0,1},{1,0},{2,3},{3,2},{4,5},{5,4},{6,7},{7,6},{8,9},{9,8},{10,11... | collective-permute-start | bytes 5308424 | tf_op jit(solution)/shard_map/ppermute | solution.py:471
  41.9 41.0 %copy-start = (f32[640,256]{1,0:T(8,128)S(1)}, f32[640,256]{1,0:T(8,128)}, u32[]{:S(2)}) copy-start(f32[640,256]{1,0:T(8,128)} %weight.3) | copy-start | bytes 1966084
  78.8 6.5 %collective-permute-start.1 = (f32[768,128]{1,0:T(8,128)S(1)}, f32[768,128]{1,0:T(8,128)S(1)}, u32[]{:S(2)}, u32[]{:S(2)}) collective-permute-start(f32[768,128]{1,0:T(8,128)S(1)} %bitcast.7), channel_id=1, source_target_pairs={{0,1},{1,0},{2,3},{3,2},{4,5},{5,4},{6,7},{7,6},{8,9},{9,8},{10,11... | collective-permute-start | bytes 1179656 | tf_op jit(solution)/shard_map/ppermute | solution.py:480

commit v6 on v5

--- a/solution.py
+++ b/solution.py
@@ -62,7 +62,6 @@
 
 
 GROUPS = (12, 14)
-META = 5
 
 
 def wanted_slots():
@@ -92,8 +91,8 @@
 
 def partial_kernel(core_of, me_of, own, *refs):
     if own:
-        acts, outgrads, prev_hbm, owner_hbm, owner_row, damping, base, homes = refs[:8]
-        out, picks, meta, buf, prev, owner, rows, sems, small_sems = refs[8:]
+        acts, outgrads, prev_hbm, owner_hbm, owner_row, damping_hbm, base, homes = refs[:8]
+        out, picks, meta, buf, prev, owner, rows, sems, small_sems, damping = refs[8:]
     else:
         acts, outgrads, prev_hbm, owner_hbm, out_hbm, buf, prev, owner, rows, sems, small_sems, out, out_sems = refs
     core, me = core_of(), me_of()
@@ -103,6 +102,9 @@
         pltpu.make_async_copy(prev_hbm, prev, small_sems.at[1]),
     ]
     small[0].start()
+    if own:
+        small.append(pltpu.make_async_copy(damping_hbm, damping, small_sems.at[2]))
+        small[2].start()
     copies = []
     for place in range(HALF):
         which, pair = pair_column(place, half)
@@ -123,9 +125,12 @@
     second_of = slot % 2
 
     if own:
+        small[2].wait()
+        lane = lax.broadcasted_iota(jnp.int32, (8, N), 1)
+        scalars = jnp.full((8, N), damping[0])
         for i, one in enumerate([block, slot_half, slot_place, second_of]):
-            meta[i] = jnp.int32(one).astype(jnp.float32)
-        meta[META - 1] = damping[0]
+            scalars = jnp.where(lane == i, jnp.int32(one).astype(jnp.float32), scalars)
+        meta[...] = scalars
         matches = (wanted_slots() == owner_row[0:1, :]).astype(jnp.float32).astype(jnp.bfloat16)
         found = jnp.dot(matches, homes[core], preferred_element_type=jnp.float32)
         picks[...] = (base[...].astype(jnp.float32) + found).astype(jnp.bfloat16)
@@ -171,19 +176,20 @@
 def partials(acts, outgrads, prev, owner, core_of, me_of, damping=None):
     own = damping is not None
     hbm, vmem = pl.BlockSpec(memory_space=pltpu.HBM), pl.BlockSpec(memory_space=pltpu.VMEM)
-    smem = pl.BlockSpec(memory_space=pltpu.SMEM)
     shape = jax.ShapeDtypeStruct((16, TILES, 8, N), jnp.float32)
     picks_shape = jax.ShapeDtypeStruct((ROWS * N, 96), jnp.bfloat16)
-    meta_shape = jax.ShapeDtypeStruct((META,), jnp.float32)
+    meta_shape = jax.ShapeDtypeStruct((8, N), jnp.float32)
     scratch = [
         pltpu.VMEM((HALF, 256, 2 * N), jnp.bfloat16),
         pltpu.VMEM((1, N, N), jnp.float32),
         pltpu.SMEM((SLOTS,), jnp.int32),
         pltpu.VMEM((N, N), jnp.float32),
         pltpu.SemaphoreType.DMA((HALF,)),
-        pltpu.SemaphoreType.DMA((2,)),
+        pltpu.SemaphoreType.DMA((3,)),
     ]
-    if not own:
+    if own:
+        scratch += [pltpu.SMEM((1,), jnp.float32)]
+    else:
         scratch += [
             pltpu.VMEM((16, TILES, 8, N), jnp.float32),
             pltpu.SemaphoreType.DMA((len(GROUPS),)),
@@ -191,8 +197,8 @@
     return pl.pallas_call(
         functools.partial(partial_kernel, core_of, me_of, own),
         out_shape=(shape, picks_shape, meta_shape) if own else shape,
-        in_specs=[hbm] * 4 + ([vmem, smem, vmem, vmem] if own else []),
-        out_specs=(vmem, vmem, smem) if own else hbm,
+        in_specs=[hbm] * 4 + ([vmem, hbm, vmem, vmem] if own else []),
+        out_specs=(vmem, vmem, vmem) if own else hbm,
         scratch_shapes=scratch,
         compiler_params=pltpu.CompilerParams(vmem_limit_bytes=(50 if own else 61) * 2**20),
         name="own_half" if own else "other_half",
@@ -355,11 +361,11 @@
 
 
 def number(meta, i):
-    return meta[i].astype(jnp.int32)
+    return meta[0, i].astype(jnp.int32)
 
 
 def near_kernel(places, meta_hbm, own, weight, rows_out, right_out, meta, meta_sem):
-    scalars = pltpu.make_async_copy(meta_hbm, meta, meta_sem.at[0])
+    scalars = pltpu.make_async_copy(meta_hbm.at[pl.ds(0, 1)], meta, meta_sem.at[0])
     scalars.start()
     core, row, col = [place() for place in places]
     group, odd_row = row // 2, row % 2
@@ -372,7 +378,7 @@
     blocks = [unpacked(first, second, diags, lane) for second in range(2)]
     blocks += [unpacked(last, second, diags, 32 * core + 10 + col // 2) for second in range(2)]
     scalars.wait()
-    approx = inverses(blocks, meta[4])
+    approx = inverses(blocks, meta[0, 4])
     right = [right_form(one) for one in approx[2:]]
     for i in range(2):
         rows_out[pl.ds(i * N, N), :] = both_sides(approx[i], weight[group_rows(2 * core + i, odd_row), :], right)
@@ -381,7 +387,7 @@
 
 def far_kernel(places, meta_hbm, own, other, weight, rows_in, right_in, out_hbm, updated_hbm, *scratch):
     out, updated, meta, meta_sem, sems = scratch
-    scalars = pltpu.make_async_copy(meta_hbm, meta, meta_sem.at[0])
+    scalars = pltpu.make_async_copy(meta_hbm.at[pl.ds(0, 1)], meta, meta_sem.at[0])
     scalars.start()
     core, row, _ = [place() for place in places]
     group, odd_row = row // 2, row % 2
@@ -411,7 +417,7 @@
     updated[0] = jnp.where(block > 0, fresh, 0.0)
     send(updated, updated_hbm)
 
-    approx = inverses(blocks, meta[4])
+    approx = inverses(blocks, meta[0, 4])
     right = [right_in[0], right_in[1]]
     for i in range(3):
         at = group_rows("fifth" if i == 2 else 2 * (1 - core) + i, odd_row)
@@ -431,7 +437,7 @@
         ),
         in_specs=[hbm, vmem, vmem],
         out_specs=(vmem, vmem),
-        scratch_shapes=[pltpu.SMEM((META,), jnp.float32), pltpu.SemaphoreType.DMA((1,))],
+        scratch_shapes=[pltpu.SMEM((1, N), jnp.float32), pltpu.SemaphoreType.DMA((1,))],
         compiler_params=pltpu.CompilerParams(vmem_limit_bytes=40 * 2**20),
         name="apply_near",
     )(meta, own, weight)
@@ -450,7 +456,7 @@
         scratch_shapes=[
             pltpu.VMEM((3 * N, 2 * N), jnp.float32),
             pltpu.VMEM((1, N, N), jnp.float32),
-            pltpu.SMEM((META,), jnp.float32),
+            pltpu.SMEM((1, N), jnp.float32),
             pltpu.SemaphoreType.DMA((1,)),
             pltpu.SemaphoreType.DMA((6,)),
         ],

time: 88.5 us -> 88 us (level)
  transfers between devices with their start and end apart: 2 -> 2, of which waited for: 0 -> 0; matrix products, arithmetic and copies ran while one was open for 0% -> 0% of each run, Pallas kernels for 7% -> 6%
where the time goes in v6:
time: 88 us; the launch traced here: 87.8 us
  blocking collectives  65.6 us (75%)
  Pallas kernels  13.4 us (15%)
  starting transfers between devices  7.48 us (8%)
  between operations  1.4 us (2%)
    all_to_all x1, blocking collectives, on_device(): lax.all_to_all(chip.reshape(16, 8 * TILES, N), PLANE, 0, 0, tiled=True)  29 us
    all_to_all x1, blocking collectives, on_device(): lax.all_to_all(sent.reshape(N, ROWS, 1, N), CHIPS, 0, 0, tiled=True)  20.5 us
    all_to_all x1, blocking collectives, on_device(): got = lax.all_to_all(by_depth, DEPTH, 0, 0, tiled=True)  16.1 us
    pallas_call x2, Pallas kernels, partials(): pl.pallas_call(functools.partial(partial_kernel, core_of, me_of, own), ou...  7.51 us
    ppermute x1, starting transfers between devices, on_device(): far = lax.ppermute(near, 'c', swap)  4.2 us
    ppermute x1, starting transfers between devices, on_device(): received = lax.ppermute(other, 'c', swap)  3.28 us
    pallas_call x1, Pallas kernels, apply_far(): pl.pallas_call(functools.partial(far_kernel, places), out_shape=(jax.Shap...  3.03 us
    pallas_call x1, Pallas kernels, apply_near(): pl.pallas_call(functools.partial(near_kernel, places), out_shape=(jax.Sha...  2.27 us
  transfers between devices with their start and end apart: 2, of which 0 were waited for; matrix products, arithmetic and copies ran while one was open for 0% of the time, Pallas kernels for 6%

profile of v6, /device:TPU:1, one launch (start us, length us, event | category | flops | bytes accessed | tf_op | source)
XLA Modules:
  0.0 87.8 jit_solution(3071356074338627047)
XLA Ops:
  0.6 0.0 copy-start.2
  0.6 0.0 copy-start.3
  0.7 0.0 copy-start.4
  0.7 0.0 copy-start.1
  0.7 4.3 %other_half.1 = f32[16,27,8,128]{3,2,1,0:T(8,128)} custom-call(bf16[256,5120]{1,0:T(8,128)(2,1)} %refs_0_.3, bf16[256,8192]{1,0:T(8,128)(2,1)} %refs_1_.3, f32[1,128,128]{2,1,0:T(8,128)} %refs_2_.3, s32[256]{0:T(256)} %refs_3_.3), custom_call_target="tpu_custom_call" | custom-call | tf_op jit(solution)/shard_map/other_half/pallas_call | solution.py:197
  5.0 3.3 %collective-permute-start = (f32[16,27,8,128]{3,2,1,0:T(8,128)}, f32[16,27,8,128]{3,2,1,0:T(8,128)S(1)}, u32[]{:S(2)}, u32[]{:S(2)}) collective-permute-start(f32[16,27,8,128]{3,2,1,0:T(8,128)} %other_half.1), channel_id=1, source_target_pairs={{0,1},{1,0},{2,3},{3,2},{4,5},{5,4},{6,7},{7,6},{8,9},{9,8},{10,11... | collective-permute-start | bytes 5308424 | tf_op jit(solution)/shard_map/ppermute | solution.py:477
  8.9 0.0 copy-done.2
  8.9 0.0 copy-done.3
  9.0 0.0 copy-done.4
  9.0 0.0 copy-done.1
  9.0 3.2 %own_half.1 = (f32[16,27,8,128]{3,2,1,0:T(8,128)S(1)}, bf16[768,96]{1,0:T(8,128)(2,1)S(1)}, f32[8,128]{1,0:T(8,128)S(1)}) custom-call(bf16[256,5120]{1,0:T(8,128)(2,1)} %refs_0_.3, bf16[256,8192]{1,0:T(8,128)(2,1)} %refs_1_.3, f32[1,128,128]{2,1,0:T(8,128)S(1)} %copy-done.1, s32[256]{0:T(256)S(1)} %copy-done.4, s32[2,128]{1,0:T(2,128)S(1)} %bitcast.11, ...), custom_call_target="tpu_custom_call" | custom-call | tf_op jit(solution)/shard_map/own_half/pallas_call | solution.py:197
  12.2 0.0 collective-permute-done.b
  12.2 0.3 add_cores.1
  12.4 29.0 %all_to_all.15.got = f32[16,216,128]{2,1,0:T(8,128)S(1)} all-to-all(f32[16,216,128]{2,1,0:T(8,128)S(1)} %bitcast.6), channel_id=1, replica_groups=mesh['zh'=2,'x'=4,'zl'=4,'y'=4,'c'=2] {'x','y'}, dimensions={0} | all-to-all | bytes 3538944 | tf_op jit(solution)/shard_map/all_to_all | solution.py:481
  41.5 0.0 copy-start
  41.5 0.1 plane_sum.1
  41.6 16.1 %all_to_all.16.got = f32[8,32,128]{2,1,0:T(8,128)S(1)} all-to-all(f32[8,32,128]{2,1,0:T(8,128)S(1)} %plane_sum.1), channel_id=1, replica_groups=mesh['zh'=2,'x'=4,'zl'=4,'y'=4,'c'=2] {'zh','zl'}, dimensions={0} | all-to-all | bytes 262144 | tf_op jit(solution)/shard_map/all_to_all | solution.py:483
  57.6 0.2 spread_rows.1
  57.8 20.5 %all_to_all.17 = f32[128,6,1,128]{3,2,1,0:T(1,128)S(1)} all-to-all(f32[128,6,1,128]{3,2,1,0:T(1,128)S(1)} %bitcast.10), channel_id=1, replica_groups=mesh['zh'=2,'x'=4,'zl'=4,'y'=4,'c'=2] {'x','y','zh','zl'}, dimensions={0} | all-to-all | bytes 786432 | tf_op jit(solution)/shard_map/all_to_all | solution.py:485
  78.3 4.2 %collective-permute-start.1 = (f32[768,128]{1,0:T(8,128)S(1)}, f32[768,128]{1,0:T(8,128)S(1)}, u32[]{:S(2)}, u32[]{:S(2)}) collective-permute-start(f32[768,128]{1,0:T(8,128)S(1)} %bitcast.7), channel_id=1, source_target_pairs={{0,1},{1,0},{2,3},{3,2},{4,5},{5,4},{6,7},{7,6},{8,9},{9,8},{10,11... | collective-permute-start | bytes 1179656 | tf_op jit(solution)/shard_map/ppermute | solution.py:486
  82.5 0.0 copy-done
  82.5 2.3 %apply_near.1 = (f32[256,256]{1,0:T(8,128)S(1)}, bf16[2,256,256]{2,1,0:T(8,128)(2,1)S(1)}) custom-call(f32[8,128]{1,0:T(8,128)S(1)} %get-tuple-element.7.meta_hbm, f32[768,128]{1,0:T(8,128)S(1)} %bitcast.8, f32[640,256]{1,0:T(8,128)S(1)} %copy-done), custom_call_target="tpu_custom_call" | custom-call | tf_op jit(solution)/shard_map/apply_near/pallas_call | solution.py:432
  84.8 0.0 collective-permute-done.1.other
  84.8 3.0 %apply_far.1 = (f32[640,256]{1,0:T(8,128)}, f32[1,128,128]{2,1,0:T(8,128)}) custom-call(f32[8,128]{1,0:T(8,128)S(1)} %get-tuple-element.7.meta_hbm, f32[768,128]{1,0:T(8,128)S(1)} %bitcast.9, f32[768,128]{1,0:T(8,128)S(1)} %collective-permute-done.1.other, f32[640,256]{1,0:T(8,128)S(1)} %copy-done, f32[256,256]{1,0:T(8,128)S(1)} %get-tuple-element.10.rows_in, ...), custom_call_target="tpu_custom_call" | custom-call | tf_op jit(solution)/shard_map/apply_far/pallas_call | solution.py:448
Async XLA Ops:
  0.6 8.3 %copy-start.2 = (bf16[768,96]{1,0:T(8,128)(2,1)S(1)}, bf16[768,96]{1,0:T(8,128)(2,1)}, u32[]{:S(2)}) copy-start(bf16[768,96]{1,0:T(8,128)(2,1)} %constant.4.clone.refs_6_) | copy-start | bytes 442372
  0.6 8.3 %copy-start.3 = (bf16[2,128,96]{2,1,0:T(8,128)(2,1)S(1)}, bf16[2,128,96]{2,1,0:T(8,128)(2,1)}, u32[]{:S(2)}) copy-start(bf16[2,128,96]{2,1,0:T(8,128)(2,1)} %constant.5.clone.refs_7_) | copy-start | bytes 147460
  0.7 8.3 %copy-start.4 = (s32[256]{0:T(256)S(1)}, s32[256]{0:T(256)}, u32[]{:S(2)}) copy-start(s32[256]{0:T(256)} %refs_3_.3) | copy-start | bytes 3076
  0.7 8.3 %copy-start.1 = (f32[1,128,128]{2,1,0:T(8,128)S(1)}, f32[1,128,128]{2,1,0:T(8,128)}, u32[]{:S(2)}) copy-start(f32[1,128,128]{2,1,0:T(8,128)} %refs_2_.3) | copy-start | bytes 196612
  5.0 7.2 %collective-permute-start = (f32[16,27,8,128]{3,2,1,0:T(8,128)}, f32[16,27,8,128]{3,2,1,0:T(8,128)S(1)}, u32[]{:S(2)}, u32[]{:S(2)}) collective-permute-start(f32[16,27,8,128]{3,2,1,0:T(8,128)} %other_half.1), channel_id=1, source_target_pairs={{0,1},{1,0},{2,3},{3,2},{4,5},{5,4},{6,7},{7,6},{8,9},{9,8},{10,11... | collective-permute-start | bytes 5308424 | tf_op jit(solution)/shard_map/ppermute | solution.py:477
  41.5 41.0 %copy-start = (f32[640,256]{1,0:T(8,128)S(1)}, f32[640,256]{1,0:T(8,128)}, u32[]{:S(2)}) copy-start(f32[640,256]{1,0:T(8,128)} %weight.3) | copy-start | bytes 1966084
  78.3 6.5 %collective-permute-start.1 = (f32[768,128]{1,0:T(8,128)S(1)}, f32[768,128]{1,0:T(8,128)S(1)}, u32[]{:S(2)}, u32[]{:S(2)}) collective-permute-start(f32[768,128]{1,0:T(8,128)S(1)} %bitcast.7), channel_id=1, source_target_pairs={{0,1},{1,0},{2,3},{3,2},{4,5},{5,4},{6,7},{7,6},{8,9},{9,8},{10,11... | collective-permute-start | bytes 1179656 | tf_op jit(solution)/shard_map/ppermute | solution.py:486

commit v7 on v6

--- a/solution.py
+++ b/solution.py
@@ -61,7 +61,7 @@
     return lax.dot_general(x, x, (((0,), (0,)), ((), ())), preferred_element_type=jnp.float32)
 
 
-GROUPS = (12, 14)
+GROUPS = (12, 10, 4)
 
 
 def wanted_slots():

time: 88 us -> 88.2 us (level)
  no operation moved by 1% of the time
where the time goes in v7:
time: 88.2 us; the launch traced here: 88 us
  blocking collectives  65.6 us (74%)
  Pallas kernels  13.5 us (15%)
  starting transfers between devices  7.53 us (9%)
  between operations  1.4 us (2%)
    all_to_all x1, blocking collectives, on_device(): lax.all_to_all(chip.reshape(16, 8 * TILES, N), PLANE, 0, 0, tiled=True)  29 us
    all_to_all x1, blocking collectives, on_device(): lax.all_to_all(sent.reshape(N, ROWS, 1, N), CHIPS, 0, 0, tiled=True)  20.5 us
    all_to_all x1, blocking collectives, on_device(): got = lax.all_to_all(by_depth, DEPTH, 0, 0, tiled=True)  16.1 us
    pallas_call x2, Pallas kernels, partials(): pl.pallas_call(functools.partial(partial_kernel, core_of, me_of, own), ou...  7.65 us
    ppermute x1, starting transfers between devices, on_device(): far = lax.ppermute(near, 'c', swap)  4.2 us
    ppermute x1, starting transfers between devices, on_device(): received = lax.ppermute(other, 'c', swap)  3.33 us
    pallas_call x1, Pallas kernels, apply_far(): pl.pallas_call(functools.partial(far_kernel, places), out_shape=(jax.Shap...  3.03 us
    pallas_call x1, Pallas kernels, apply_near(): pl.pallas_call(functools.partial(near_kernel, places), out_shape=(jax.Sha...  2.27 us
  transfers between devices with their start and end apart: 2, of which 0 were waited for; matrix products, arithmetic and copies ran while one was open for 0% of the time, Pallas kernels for 6%

profile of v7, /device:TPU:1, one launch (start us, length us, event | category | flops | bytes accessed | tf_op | source)
XLA Modules:
  0.0 88.0 jit_solution(9002752745364363153)
XLA Ops:
  0.6 0.0 copy-start.2
  0.6 0.0 copy-start.3
  0.7 0.0 copy-start.4
  0.7 0.0 copy-start.1
  0.7 4.3 %other_half.1 = f32[16,27,8,128]{3,2,1,0:T(8,128)} custom-call(bf16[256,5120]{1,0:T(8,128)(2,1)} %refs_0_.3, bf16[256,8192]{1,0:T(8,128)(2,1)} %refs_1_.3, f32[1,128,128]{2,1,0:T(8,128)} %refs_2_.3, s32[256]{0:T(256)} %refs_3_.3), custom_call_target="tpu_custom_call" | custom-call | tf_op jit(solution)/shard_map/other_half/pallas_call | solution.py:197
  4.9 3.3 %collective-permute-start = (f32[16,27,8,128]{3,2,1,0:T(8,128)}, f32[16,27,8,128]{3,2,1,0:T(8,128)S(1)}, u32[]{:S(2)}, u32[]{:S(2)}) collective-permute-start(f32[16,27,8,128]{3,2,1,0:T(8,128)} %other_half.1), channel_id=1, source_target_pairs={{0,1},{1,0},{2,3},{3,2},{4,5},{5,4},{6,7},{7,6},{8,9},{9,8},{10,11... | collective-permute-start | bytes 5308424 | tf_op jit(solution)/shard_map/ppermute | solution.py:477
  8.9 0.0 copy-done.2
  8.9 0.0 copy-done.3
  8.9 0.0 copy-done.4
  9.0 0.0 copy-done.1
  9.0 3.4 %own_half.1 = (f32[16,27,8,128]{3,2,1,0:T(8,128)S(1)}, bf16[768,96]{1,0:T(8,128)(2,1)S(1)}, f32[8,128]{1,0:T(8,128)S(1)}) custom-call(bf16[256,5120]{1,0:T(8,128)(2,1)} %refs_0_.3, bf16[256,8192]{1,0:T(8,128)(2,1)} %refs_1_.3, f32[1,128,128]{2,1,0:T(8,128)S(1)} %copy-done.1, s32[256]{0:T(256)S(1)} %copy-done.4, s32[2,128]{1,0:T(2,128)S(1)} %bitcast.11, ...), custom_call_target="tpu_custom_call" | custom-call | tf_op jit(solution)/shard_map/own_half/pallas_call | solution.py:197
  12.4 0.0 collective-permute-done.b
  12.4 0.3 add_cores.1
  12.6 29.0 %all_to_all.15.got = f32[16,216,128]{2,1,0:T(8,128)S(1)} all-to-all(f32[16,216,128]{2,1,0:T(8,128)S(1)} %bitcast.6), channel_id=1, replica_groups=mesh['zh'=2,'x'=4,'zl'=4,'y'=4,'c'=2] {'x','y'}, dimensions={0} | all-to-all | bytes 3538944 | tf_op jit(solution)/shard_map/all_to_all | solution.py:481
  41.6 0.0 copy-start
  41.6 0.1 plane_sum.1
  41.7 16.1 %all_to_all.16.got = f32[8,32,128]{2,1,0:T(8,128)S(1)} all-to-all(f32[8,32,128]{2,1,0:T(8,128)S(1)} %plane_sum.1), channel_id=1, replica_groups=mesh['zh'=2,'x'=4,'zl'=4,'y'=4,'c'=2] {'zh','zl'}, dimensions={0} | all-to-all | bytes 262144 | tf_op jit(solution)/shard_map/all_to_all | solution.py:483
  57.8 0.2 spread_rows.1
  58.0 20.5 %all_to_all.17 = f32[128,6,1,128]{3,2,1,0:T(1,128)S(1)} all-to-all(f32[128,6,1,128]{3,2,1,0:T(1,128)S(1)} %bitcast.10), channel_id=1, replica_groups=mesh['zh'=2,'x'=4,'zl'=4,'y'=4,'c'=2] {'x','y','zh','zl'}, dimensions={0} | all-to-all | bytes 786432 | tf_op jit(solution)/shard_map/all_to_all | solution.py:485
  78.5 4.2 %collective-permute-start.1 = (f32[768,128]{1,0:T(8,128)S(1)}, f32[768,128]{1,0:T(8,128)S(1)}, u32[]{:S(2)}, u32[]{:S(2)}) collective-permute-start(f32[768,128]{1,0:T(8,128)S(1)} %bitcast.7), channel_id=1, source_target_pairs={{0,1},{1,0},{2,3},{3,2},{4,5},{5,4},{6,7},{7,6},{8,9},{9,8},{10,11... | collective-permute-start | bytes 1179656 | tf_op jit(solution)/shard_map/ppermute | solution.py:486
  82.7 0.0 copy-done
  82.7 2.3 %apply_near.1 = (f32[256,256]{1,0:T(8,128)S(1)}, bf16[2,256,256]{2,1,0:T(8,128)(2,1)S(1)}) custom-call(f32[8,128]{1,0:T(8,128)S(1)} %get-tuple-element.7.meta_hbm, f32[768,128]{1,0:T(8,128)S(1)} %bitcast.8, f32[640,256]{1,0:T(8,128)S(1)} %copy-done), custom_call_target="tpu_custom_call" | custom-call | tf_op jit(solution)/shard_map/apply_near/pallas_call | solution.py:432
  85.0 0.0 collective-permute-done.1.other
  85.0 3.0 %apply_far.1 = (f32[640,256]{1,0:T(8,128)}, f32[1,128,128]{2,1,0:T(8,128)}) custom-call(f32[8,128]{1,0:T(8,128)S(1)} %get-tuple-element.7.meta_hbm, f32[768,128]{1,0:T(8,128)S(1)} %bitcast.9, f32[768,128]{1,0:T(8,128)S(1)} %collective-permute-done.1.other, f32[640,256]{1,0:T(8,128)S(1)} %copy-done, f32[256,256]{1,0:T(8,128)S(1)} %get-tuple-element.10.rows_in, ...), custom_call_target="tpu_custom_call" | custom-call | tf_op jit(solution)/shard_map/apply_far/pallas_call | solution.py:448
Async XLA Ops:
  0.6 8.3 %copy-start.2 = (bf16[768,96]{1,0:T(8,128)(2,1)S(1)}, bf16[768,96]{1,0:T(8,128)(2,1)}, u32[]{:S(2)}) copy-start(bf16[768,96]{1,0:T(8,128)(2,1)} %constant.4.clone.refs_6_) | copy-start | bytes 442372
  0.6 8.3 %copy-start.3 = (bf16[2,128,96]{2,1,0:T(8,128)(2,1)S(1)}, bf16[2,128,96]{2,1,0:T(8,128)(2,1)}, u32[]{:S(2)}) copy-start(bf16[2,128,96]{2,1,0:T(8,128)(2,1)} %constant.5.clone.refs_7_) | copy-start | bytes 147460
  0.7 8.3 %copy-start.4 = (s32[256]{0:T(256)S(1)}, s32[256]{0:T(256)}, u32[]{:S(2)}) copy-start(s32[256]{0:T(256)} %refs_3_.3) | copy-start | bytes 3076
  0.7 8.3 %copy-start.1 = (f32[1,128,128]{2,1,0:T(8,128)S(1)}, f32[1,128,128]{2,1,0:T(8,128)}, u32[]{:S(2)}) copy-start(f32[1,128,128]{2,1,0:T(8,128)} %refs_2_.3) | copy-start | bytes 196612
  4.9 7.4 %collective-permute-start = (f32[16,27,8,128]{3,2,1,0:T(8,128)}, f32[16,27,8,128]{3,2,1,0:T(8,128)S(1)}, u32[]{:S(2)}, u32[]{:S(2)}) collective-permute-start(f32[16,27,8,128]{3,2,1,0:T(8,128)} %other_half.1), channel_id=1, source_target_pairs={{0,1},{1,0},{2,3},{3,2},{4,5},{5,4},{6,7},{7,6},{8,9},{9,8},{10,11... | collective-permute-start | bytes 5308424 | tf_op jit(solution)/shard_map/ppermute | solution.py:477
  41.6 41.1 %copy-start = (f32[640,256]{1,0:T(8,128)S(1)}, f32[640,256]{1,0:T(8,128)}, u32[]{:S(2)}) copy-start(f32[640,256]{1,0:T(8,128)} %weight.3) | copy-start | bytes 1966084
  78.5 6.5 %collective-permute-start.1 = (f32[768,128]{1,0:T(8,128)S(1)}, f32[768,128]{1,0:T(8,128)S(1)}, u32[]{:S(2)}, u32[]{:S(2)}) collective-permute-start(f32[768,128]{1,0:T(8,128)S(1)} %bitcast.7), channel_id=1, source_target_pairs={{0,1},{1,0},{2,3},{3,2},{4,5},{5,4},{6,7},{7,6},{8,9},{9,8},{10,11... | collective-permute-start | bytes 1179656 | tf_op jit(solution)/shard_map/ppermute | solution.py:486
